TPU v7x, 512 devices: a whole 4x4x16 slice. The times are simulated.
512 devices in a mesh: row: 8 (over x, core), col: 4 (over y), gz: 16 (over z).
Axes of the slice: x: 4, y: 4, z: 16, core: 2. Of those that a mesh axis runs over, the one named last changes fastest.
Arguments:
- parent: int32 [64], P('gz'), may hold values from 0 to 3, as said below
- l_tree: bfloat16 [64, 256, 256], P('gz', 'row', 'col'), may hold values from -0.375 to 0.375
- l_path: bfloat16 [128, 4, 256, 256], P('gz', None, 'row', 'col'), may hold values from -0.09375 to 0.09375
- l_top: bfloat16 [15, 4, 256, 256], P(None, None, 'row', 'col'), may hold values from -0.25 to 0.25
- u_tree: bfloat16 [64, 256, 256], P('gz', 'col', 'row'), may hold values from -0.375 to 0.375
- u_path: bfloat16 [128, 4, 256, 256], P('gz', None, 'col', 'row'), may hold values from -0.1875 to 0.1875
- u_top: bfloat16 [15, 4, 256, 256], P(None, None, 'col', 'row'), may hold values from -0.1875 to 0.1875
- linv_local: bfloat16 [128, 256, 256], P('gz', 'col'), may hold values from -0.375 to 0.375
- linv_top: bfloat16 [15, 256, 256], P(None, 'col'), may hold values from -0.375 to 0.375
- uinv_local: bfloat16 [128, 256, 256], P('gz', 'row'), may hold values from -0.375 to 0.375
- uinv_top: bfloat16 [15, 256, 256], P(None, 'row'), may hold values from -0.375 to 0.375
- rhs_local: bfloat16 [128, 256, 512], P('gz', 'row'), may hold values from -6 to 6
- rhs_top: bfloat16 [15, 256, 512], P(None, 'row'), may hold values from -6 to 6
Outputs:
- x_local: float32 [128, 256, 512], P('gz', ('row', 'col'))
- x_path: float32 [16, 4, 256, 512], P('gz', None, ('row', 'col'))
Inputs may be any that keep to these rules, and one draw needn't show every extreme that they name: Entry g * 4 + j names, within layer g, the level-one parent of level-zero supernode j; in every layer some supernode has parent 0 and some has parent 4 - 1.
All inputs are finite; a program needn't handle non-finite values.
Results may differ from a plain program's by a relative error of at most 0.04.
Values may be sent and summed in bfloat16 or wider, within the bound.
A program may use at most 64 MiB of HBM per device.

v0:
```python
import jax
import jax.numpy as jnp
from jax import lax
from jax.sharding import PartitionSpec as P


def blocks_layout(
    parent,
    l_tree,
    l_path,
    l_top,
    u_tree,
    u_path,
    u_top,
    linv_local,
    linv_top,
    uinv_local,
    uinv_top,
    rhs_local,
    rhs_top,
):
    row_count = lax.axis_size("row")
    col_count = lax.axis_size("col")
    layers = lax.axis_size("gz")
    levels = layers.bit_length() - 1
    layer_index = lax.axis_index("gz")
    row_index = lax.axis_index("row")
    col_index = lax.axis_index("col")
    per_level = parent.shape[0]
    total_top = l_top.shape[0]
    seg_rows = rhs_local.shape[1]
    piece_rows = seg_rows // col_count

    def apply_inverse(inverse, gathered):
        return jnp.einsum("nab,nbr->nar", inverse, gathered, preferred_element_type=jnp.float32)

    def broadcast_rows(values):
        return lax.all_gather(values, "row", axis=1, tiled=True)

    def permuted(inverse):
        block_count = inverse.shape[0]
        inner = inverse.shape[1]
        shaped = inverse.reshape(block_count, inner, col_count, row_count, piece_rows)
        return shaped.transpose(0, 1, 3, 2, 4).reshape(block_count, inner, -1)

    def back_solve(upper_y, partial_value, inverse):
        own_share = lax.dynamic_slice_in_dim(upper_y, row_index * piece_rows, piece_rows, 1)
        if partial_value is not None:
            own_share = own_share - lax.psum_scatter(
                partial_value.astype(jnp.bfloat16), "row", scatter_dimension=1, tiled=True
            ).astype(jnp.float32)
        gathered = lax.all_gather(
            own_share.astype(jnp.bfloat16), ("row", "col"), axis=1, tiled=True
        )
        return jnp.einsum(
            "nab,nbr->nar", permuted(inverse), gathered, preferred_element_type=jnp.float32
        )

    first_full = broadcast_rows(rhs_local[:per_level])
    first_y = apply_inverse(linv_local[:per_level], first_full)
    first_low = first_y.astype(jnp.bfloat16)
    forwarded_values = jnp.einsum(
        "jab,jbr->jar", l_tree, first_low, preferred_element_type=jnp.float32
    )
    select_option = (parent[:, None] == jnp.arange(per_level, dtype=jnp.int32)[None, :]).astype(
        jnp.float32
    )
    collected_terms = jnp.einsum("no,nvk->ovk", select_option, forwarded_values)
    second_rhs = rhs_local[per_level:]
    summed = lax.psum(collected_terms.astype(jnp.bfloat16), "col").astype(jnp.float32)
    second_full = broadcast_rows((second_rhs.astype(jnp.float32) - summed).astype(jnp.bfloat16))
    second_y = apply_inverse(linv_local[per_level:], second_full)
    local_low = jnp.concatenate([first_y, second_y], 0).astype(jnp.bfloat16)
    toward = jnp.einsum("kmab,kbr->mar", l_path, local_low, preferred_element_type=jnp.float32)
    ancestor_ids = [
        layers - (layers >> depth) + layer_index // 2 ** (depth + 1) for depth in range(levels)
    ]
    id_stack = jnp.stack(ancestor_ids)
    place_table = (id_stack[:, None] == jnp.arange(total_top, dtype=jnp.int32)[None, :]).astype(
        jnp.float32
    )
    toward = lax.psum(toward.astype(jnp.bfloat16), "col").astype(jnp.float32)
    spread_all = jnp.einsum("mn,mar->nar", place_table, toward)
    everything = lax.psum(spread_all.astype(jnp.bfloat16), "gz").astype(jnp.float32)
    picked = jnp.einsum("mn,nar->mar", place_table, everything)
    pending = [picked[depth] for depth in range(levels)]
    path_y = []
    for tree_level in range(levels):
        node_id = ancestor_ids[tree_level]
        rhs_now = lax.dynamic_index_in_dim(rhs_top, node_id, 0, keepdims=True)
        target_rows = (rhs_now.astype(jnp.float32) - pending[tree_level][None]).astype(jnp.bfloat16)
        full_rhs = broadcast_rows(target_rows)
        inverse = lax.dynamic_index_in_dim(linv_top, node_id, 0, keepdims=True)
        solved = apply_inverse(inverse, full_rhs)
        path_y.append(solved)
        if tree_level + 1 < levels:
            blocks = lax.dynamic_index_in_dim(l_top, node_id, 0, keepdims=False)[tree_level + 1 :]
            lead_mask = (layer_index % 2 ** (tree_level + 1) == 0).astype(jnp.float32)
            upward = (
                jnp.einsum(
                    "mab,br->mar",
                    blocks,
                    solved[0].astype(jnp.bfloat16),
                    preferred_element_type=jnp.float32,
                )
                * lead_mask
            )
            first_upper = layers - (layers >> tree_level + 1)
            slot_count = total_top - first_upper
            target_ids = id_stack[tree_level + 1 :] - first_upper
            spot_table = (
                target_ids[:, None] == jnp.arange(slot_count, dtype=jnp.int32)[None, :]
            ).astype(jnp.float32)
            upper_sum = lax.psum(jnp.einsum("mn,mar->nar", spot_table, upward), ("col", "gz"))
            arrived = jnp.einsum("mn,nar->mar", spot_table, upper_sum)
            for offset in range(levels - tree_level - 1):
                pending[tree_level + 1 + offset] = (
                    pending[tree_level + 1 + offset] + arrived[offset]
                )
    path_x = [None] * levels
    for tree_level in reversed(range(levels)):
        node_id = ancestor_ids[tree_level]
        partial_value = None
        if tree_level + 1 < levels:
            blocks = lax.dynamic_index_in_dim(u_top, node_id, 0, keepdims=False)[tree_level + 1 :]
            above = jnp.concatenate(path_x[tree_level + 1 :], 0).astype(jnp.bfloat16)
            partial_value = jnp.einsum(
                "mab,mbr->ar", blocks, above, preferred_element_type=jnp.float32
            )[None]
        inverse = lax.dynamic_index_in_dim(uinv_top, node_id, 0, keepdims=True)
        path_x[tree_level] = back_solve(path_y[tree_level], partial_value, inverse)
    path_stack = jnp.concatenate(path_x, 0)
    path_low = path_stack.astype(jnp.bfloat16)
    path_term = jnp.einsum("kmab,mbr->kar", u_path, path_low, preferred_element_type=jnp.float32)
    second_x = back_solve(second_y, path_term[per_level:], uinv_local[per_level:])
    parent_low = jnp.einsum(
        "ey,yuf->euf",
        select_option.astype(jnp.bfloat16),
        second_x.astype(jnp.bfloat16),
        preferred_element_type=jnp.float32,
    ).astype(jnp.bfloat16)
    tree_term = jnp.einsum("jab,jbr->jar", u_tree, parent_low, preferred_element_type=jnp.float32)
    first_x = back_solve(first_y, path_term[:per_level] + tree_term, uinv_local[:per_level])
    x_all = jnp.concatenate([first_x, second_x], 0)
    x_local = lax.dynamic_slice_in_dim(x_all, col_index * piece_rows, piece_rows, 1)
    x_path = lax.dynamic_slice_in_dim(path_stack, col_index * piece_rows, piece_rows, 1)[None]
    return (x_local, x_path)


def per_device(
    parent,
    l_tree,
    l_path,
    l_top,
    u_tree,
    u_path,
    u_top,
    linv_local,
    linv_top,
    uinv_local,
    uinv_top,
    rhs_local,
    rhs_top,
):
    return blocks_layout(
        parent,
        l_tree,
        l_path,
        l_top,
        u_tree,
        u_path,
        u_top,
        linv_local,
        linv_top,
        uinv_local,
        uinv_top,
        rhs_local,
        rhs_top,
    )


def solution(mesh):
    placed = (
        P("gz"),
        P("gz", "row", "col"),
        P("gz", None, "row", "col"),
        P(None, None, "row", "col"),
        P("gz", "col", "row"),
        P("gz", None, "col", "row"),
        P(None, None, "col", "row"),
        P("gz", "col", None),
        P(None, "col", None),
        P("gz", "row", None),
        P(None, "row", None),
        P("gz", "row", None),
        P(None, "row", None),
    )
    return jax.shard_map(
        per_device,
        mesh=mesh,
        in_specs=placed,
        out_specs=(P("gz", ("row", "col"), None), P("gz", None, ("row", "col"), None)),
        check_vma=False,
    )
```

profile of v0, /device:TPU:1, one launch (start us, length us, event | category | flops | bytes accessed | tf_op | source)
XLA Modules:
  0.0 1700.6 jit_solution(11898192892556224136)
XLA Ops:
  7.2 1.7 fusion.112
  9.0 38.6 %all-gather.6.cloned.1.call-done = bf16[4,256,512]{2,1,0:T(8,128)(2,1)} async-done(((bf16[4,32,512]{2,1,0:T(8,128)(2,1)}), bf16[4,256,512]{2,1,0:T(8,128)(2,1)}) %all-gather.6.cloned.1.call-update) | async-done | bytes 1048592 | tf_op jit(solution)/shard_map/all_gather | solution.py:38
  47.7 1.5 fusion.115
  49.4 0.5 copy-done.7
  49.9 1.0 convolution_convert_fusion.1
  50.9 54.0 %all-reduce.7.cloned.1.call-done = bf16[4,32,512]{2,0,1:T(4,128)(2,1)} async-done(((bf16[4,32,512]{2,0,1:T(4,128)(2,1)}), bf16[4,32,512]{2,0,1:T(4,128)(2,1)}) %all-reduce.7.cloned.1.call-update) | async-done | bytes 131088 | tf_op jit(solution)/shard_map/psum | solution.py:70
  104.9 1.7 subtract_convert_fusion
  106.7 35.4 %all-gather.8.cloned.1.call-done = bf16[4,256,512]{2,0,1:T(4,128)(2,1)} async-done(((bf16[4,32,512]{2,0,1:T(4,128)(2,1)}), bf16[4,256,512]{2,0,1:T(4,128)(2,1)}) %all-gather.8.cloned.1.call-update) | async-done | bytes 1048592 | tf_op jit(solution)/shard_map/all_gather | solution.py:38
  142.0 1.6 fusion.11
  143.8 0.9 copy-done.6
  144.7 0.9 fusion.3
  145.8 53.9 %all-reduce.9.cloned.1.call-done = bf16[4,32,512]{2,1,0:T(8,128)(2,1)} async-done(((bf16[4,32,512]{2,1,0:T(8,128)(2,1)}), bf16[4,32,512]{2,1,0:T(8,128)(2,1)}) %all-reduce.9.cloned.1.call-update) | async-done | bytes 131088 | tf_op jit(solution)/shard_map/psum | solution.py:82
  199.7 2.2 convolution_convert_fusion
  202.1 129.6 %all-reduce.11.cloned.1.call-done = bf16[15,32,512]{2,0,1:T(8,128)(2,1)} async-done(((bf16[15,32,512]{2,0,1:T(8,128)(2,1)}), bf16[15,32,512]{2,0,1:T(8,128)(2,1)}) %all-reduce.11.cloned.1.call-update) | async-done | bytes 491536 | tf_op jit(solution)/shard_map/psum | solution.py:84
  331.8 1.3 fusion.94
  333.3 0.8 fusion.55
  334.0 23.1 %all_gather.38 = bf16[1,256,512]{2,1,0:T(8,128)(2,1)S(1)} all-gather(bf16[1,32,512]{2,1,0:T(8,128)(2,1)S(1)} %fusion.55), channel_id=1, replica_groups=mesh['row'=8,'col'=4,'gz'=16] {'row'}, dimensions={1}, use_global_device_ids=true | all-gather | bytes 294912 | tf_op jit(solution)/shard_map/all_gather | solution.py:38
  357.3 0.9 convolution_multiply_fusion
  358.2 0.3 fusion.28
  358.6 226.1 %all-reduce.14 = bf16[7,32,512]{2,0,1:T(8,128)(2,1)S(1)} all-reduce(f32[7,32,512]{2,0,1:T(8,128)S(1)} %fusion.28), channel_id=1, replica_groups=mesh['row'=8,'col'=4,'gz'=16] {'col','gz'}, use_global_device_ids=true, to_apply=%region_3.4 | all-reduce | flops 114688 | bytes 688128 | tf_op jit(solution)/shard_map/psum | solution.py:114
  584.7 0.3 fusion.91
  585.1 0.8 fusion.54
  585.9 68.1 %all_gather.39 = bf16[1,256,512]{2,1,0:T(8,128)(2,1)S(1)} all-gather(bf16[1,32,512]{2,1,0:T(8,128)(2,1)S(1)} %fusion.54), channel_id=1, replica_groups=mesh['row'=8,'col'=4,'gz'=16] {'row'}, dimensions={1}, use_global_device_ids=true | all-gather | bytes 294912 | tf_op jit(solution)/shard_map/all_gather | solution.py:38
  654.2 0.9 convolution_multiply_fusion.1
  655.0 0.3 fusion.35
  655.4 219.4 %all-reduce.15 = bf16[3,32,512]{2,0,1:T(4,128)(2,1)S(1)} all-reduce(f32[3,32,512]{2,0,1:T(4,128)S(1)} %fusion.35), channel_id=1, replica_groups=mesh['row'=8,'col'=4,'gz'=16] {'col','gz'}, use_global_device_ids=true, to_apply=%region_4.5 | all-reduce | flops 49152 | bytes 294912 | tf_op jit(solution)/shard_map/psum | solution.py:114
  875.1 0.8 fusion.52
  875.9 67.5 %all_gather.40 = bf16[1,256,512]{2,1,0:T(8,128)(2,1)S(1)} all-gather(bf16[1,32,512]{2,1,0:T(8,128)(2,1)S(1)} %fusion.52), channel_id=1, replica_groups=mesh['row'=8,'col'=4,'gz'=16] {'row'}, dimensions={1}, use_global_device_ids=true | all-gather | bytes 294912 | tf_op jit(solution)/shard_map/all_gather | solution.py:38
  943.6 1.5 fusion.10
  945.1 0.8 constant_dynamic-slice_fusion.3
  946.0 234.0 %all-reduce.13.cloned.1.call-done = f32[1,32,512]{2,1,0:T(8,128)} async-done(((f32[1,32,512]{2,1,0:T(8,128)}), f32[1,32,512]{2,1,0:T(8,128)}) %all-reduce.13.cloned.1.call-update) | async-done | bytes 65552 | tf_op jit(solution)/shard_map/psum | solution.py:114
  1180.1 0.9 fusion.50
  1180.9 23.9 %all_gather.41 = bf16[1,256,512]{2,1,0:T(8,128)(2,1)S(1)} all-gather(bf16[1,32,512]{2,1,0:T(8,128)(2,1)S(1)} %fusion.50), channel_id=1, replica_groups=mesh['row'=8,'col'=4,'gz'=16] {'row'}, dimensions={1}, use_global_device_ids=true | all-gather | bytes 294912 | tf_op jit(solution)/shard_map/all_gather | solution.py:38
  1205.0 41.6 %all-gather = bf16[256,512]{1,0:T(8,128)(2,1)S(1)} all-gather(bf16[8,512]{1,0:T(8,128)(2,1)S(1)} %dynamic-slice_convert_fusion), channel_id=2, replica_groups=mesh['row'=8,'col'=4,'gz'=16] {'row','col'}, dimensions={0}, use_global_device_ids=true | all-gather | bytes 270336 | tf_op jit(solution)/shard_map/all_gather | solution.py:52
  1246.8 1.5 fusion.6
  1248.6 29.0 %reduce-scatter.10.cloned.1.call-done = bf16[1,8,512]{2,1,0:T(8,128)(2,1)} async-done(((bf16[1,64,512]{2,1,0:T(8,128)(2,1)}), bf16[1,8,512]{2,1,0:T(8,128)(2,1)}) %reduce-scatter.10.cloned.1.call-update) | async-done | bytes 8208 | tf_op jit(solution)/shard_map/reduce_scatter | solution.py:49
  1277.5 0.7 fusion.71
  1278.2 43.1 %all_gather.43 = bf16[1,256,512]{2,1,0:T(8,128)(2,1)S(1)} all-gather(bf16[1,8,512]{2,1,0:T(8,128)(2,1)S(1)} %fusion.71), channel_id=1, replica_groups=mesh['row'=8,'col'=4,'gz'=16] {'row','col'}, dimensions={1}, use_global_device_ids=true | all-gather | bytes 270336 | tf_op jit(solution)/shard_map/all_gather | solution.py:52
  1321.5 1.5 fusion.8
  1323.2 36.9 %reduce-scatter.12.cloned.1.call-done = bf16[1,8,512]{2,1,0:T(8,128)(2,1)} async-done(((bf16[1,64,512]{2,1,0:T(8,128)(2,1)}), bf16[1,8,512]{2,1,0:T(8,128)(2,1)}) %reduce-scatter.12.cloned.1.call-update) | async-done | bytes 8208 | tf_op jit(solution)/shard_map/reduce_scatter | solution.py:49
  1360.1 0.7 fusion.72
  1360.8 43.1 %all_gather.44 = bf16[1,256,512]{2,1,0:T(8,128)(2,1)S(1)} all-gather(bf16[1,8,512]{2,1,0:T(8,128)(2,1)S(1)} %fusion.72), channel_id=1, replica_groups=mesh['row'=8,'col'=4,'gz'=16] {'row','col'}, dimensions={1}, use_global_device_ids=true | all-gather | bytes 270336 | tf_op jit(solution)/shard_map/all_gather | solution.py:52
  1404.1 1.6 fusion.7
  1405.9 37.0 %reduce-scatter.14.cloned.1.call-done = bf16[1,8,512]{2,1,0:T(8,128)(2,1)} async-done(((bf16[1,64,512]{2,1,0:T(8,128)(2,1)}), bf16[1,8,512]{2,1,0:T(8,128)(2,1)}) %reduce-scatter.14.cloned.1.call-update) | async-done | bytes 8208 | tf_op jit(solution)/shard_map/reduce_scatter | solution.py:49
  1442.9 0.7 fusion.73
  1443.6 43.1 %all_gather.45 = bf16[1,256,512]{2,1,0:T(8,128)(2,1)S(1)} all-gather(bf16[1,8,512]{2,1,0:T(8,128)(2,1)S(1)} %fusion.73), channel_id=1, replica_groups=mesh['row'=8,'col'=4,'gz'=16] {'row','col'}, dimensions={1}, use_global_device_ids=true | all-gather | bytes 270336 | tf_op jit(solution)/shard_map/all_gather | solution.py:52
  1486.8 0.8 copy-done.2
  1487.6 0.3 convolution_bitcast_fusion
  1488.2 0.8 copy.162
  1489.0 37.4 %reduce-scatter.16.cloned.1.call-done = bf16[8,2048]{1,0:T(8,128)(2,1)} async-done(((bf16[64,2048]{1,0:T(8,128)(2,1)}), bf16[8,2048]{1,0:T(8,128)(2,1)}) %reduce-scatter.16.cloned.1.call-update) | async-done | bytes 32784
  1526.4 0.8 reshape.193
  1527.2 0.6 fusion.56
  1528.1 61.5 %all-gather.10.cloned.1.call-done = bf16[4,256,512]{2,1,0:T(8,128)(2,1)} async-done(((bf16[4,8,512]{2,1,0:T(8,128)(2,1)}), bf16[4,256,512]{2,1,0:T(8,128)(2,1)}) %all-gather.10.cloned.1.call-update) | async-done | bytes 1048592 | tf_op jit(solution)/shard_map/all_gather | solution.py:52
  1589.7 1.5 fusion.118
  1591.2 0.3 convolution_convert_fusion.2
  1591.5 0.5 copy-done.5
  1592.5 0.8 copy.163
  1593.3 35.8 %reduce-scatter.18.cloned.1.call-done = bf16[8,2048]{1,0:T(8,128)(2,1)} async-done(((bf16[64,2048]{1,0:T(8,128)(2,1)}), bf16[8,2048]{1,0:T(8,128)(2,1)}) %reduce-scatter.18.cloned.1.call-update) | async-done | bytes 32784
  1629.0 0.8 reshape.195
  1629.8 0.6 subtract_convert_fusion.1
  1630.7 0.6 dynamic-slice_bitcast_fusion
  1631.4 60.5 %all-gather.12.cloned.1.call-done = bf16[4,256,512]{2,1,0:T(8,128)(2,1)} async-done(((bf16[4,8,512]{2,1,0:T(8,128)(2,1)}), bf16[4,256,512]{2,1,0:T(8,128)(2,1)}) %all-gather.12.cloned.1.call-update) | async-done | bytes 1048592 | tf_op jit(solution)/shard_map/all_gather | solution.py:52
  1691.9 1.5 convolution_bitcast_fusion.4
  1693.4 0.7 fusion.31
  (74 shorter events, 4.9 us)
Async XLA Ops:
  7.2 350.0 %copy-start = (bf16[15,64,256]{2,1,0:T(8,128)(2,1)S(1)}, bf16[15,64,256]{2,1,0:T(8,128)(2,1)}, u32[]{:S(2)}) copy-start(bf16[15,64,256]{2,1,0:T(8,128)(2,1)} %param.21) | copy-start | bytes 1474564
  7.2 40.5 %copy-start.1 = (bf16[8,64,256]{2,1,0:T(8,128)(2,1)S(1)}, bf16[8,64,256]{2,1,0:T(8,128)(2,1)}, u32[]{:S(2)}) copy-start(bf16[8,64,256]{2,1,0:T(8,128)(2,1)} %param.20) | copy-start | bytes 786436
  7.2 40.5 %all-gather.6.cloned.1.call-start = ((), (), s32[]{:S(2)}) async-start(), calls=%async_computation.5 | async-start | bytes 1179648 | tf_op jit(solution)/shard_map/all_gather | solution.py:38
  9.0 40.2 %copy-start.4 = (bf16[4,32,64]{2,1,0:T(8,128)(2,1)S(1)}, bf16[4,32,64]{2,1,0:T(8,128)(2,1)}, u32[]{:S(2)}) copy-start(bf16[4,32,64]{2,1,0:T(8,128)(2,1)} %param.14) | copy-start | bytes 49156
  9.0 95.9 %all-reduce.7.cloned.1.call-start = ((), (), s32[]{:S(2)}) async-start(), calls=%async_computation.6 | async-start | bytes 262144 | tf_op jit(solution)/shard_map/psum | solution.py:70
  49.2 0.7 copy-start.7
  50.9 91.2 %all-gather.8.cloned.1.call-start = ((), (), s32[]{:S(2)}) async-start(), calls=%async_computation.7 | async-start | bytes 1179648 | tf_op jit(solution)/shard_map/all_gather | solution.py:38
  106.6 93.0 %all-reduce.9.cloned.1.call-start = ((), (), s32[]{:S(2)}) async-start(), calls=%async_computation.8 | async-start | bytes 262144 | tf_op jit(solution)/shard_map/psum | solution.py:82
  143.7 1.0 copy-start.6
  145.6 186.1 %all-reduce.11.cloned.1.call-start = ((), (), s32[]{:S(2)}) async-start(), calls=%async_computation.9 | async-start | bytes 1048576 | tf_op jit(solution)/shard_map/psum | solution.py:84
  201.8 978.2 %all-reduce.13.cloned.1.call-start = ((), (), s32[]{:S(2)}) async-start(), calls=%async_computation.10 | async-start | bytes 131072 | tf_op jit(solution)/shard_map/psum | solution.py:114
  945.0 332.5 %reduce-scatter.10.cloned.1.call-start = ((), (), s32[]{:S(2)}) async-start(), calls=%async_computation.11 | async-start | bytes 73728 | tf_op jit(solution)/shard_map/reduce_scatter | solution.py:49
  1248.4 111.8 %reduce-scatter.12.cloned.1.call-start = ((), (), s32[]{:S(2)}) async-start(), calls=%async_computation.12 | async-start | bytes 73728 | tf_op jit(solution)/shard_map/reduce_scatter | solution.py:49
  1323.0 119.8 %reduce-scatter.14.cloned.1.call-start = ((), (), s32[]{:S(2)}) async-start(), calls=%async_computation.13 | async-start | bytes 73728 | tf_op jit(solution)/shard_map/reduce_scatter | solution.py:49
  1405.7 120.7 %reduce-scatter.16.cloned.1.call-start = ((), (), s32[]{:S(2)}) async-start(), calls=%async_computation.16 | async-start | bytes 294912
  1486.6 1.0 copy-start.2
  1489.0 38.9 %copy-start.3 = (bf16[8,32,256]{2,1,0:T(8,128)(2,1)S(1)}, bf16[8,32,256]{2,1,0:T(8,128)(2,1)}, u32[]{:S(2)}) copy-start(bf16[8,32,256]{2,1,0:T(8,128)(2,1)} %param.22) | copy-start | bytes 393220
  1489.0 100.7 %all-gather.10.cloned.1.call-start = ((), (), s32[]{:S(2)}) async-start(), calls=%async_computation.14 | async-start | bytes 1081344 | tf_op jit(solution)/shard_map/all_gather | solution.py:52
  1527.8 101.2 %reduce-scatter.18.cloned.1.call-start = ((), (), s32[]{:S(2)}) async-start(), calls=%async_computation.17 | async-start | bytes 294912
  1591.2 0.8 copy-start.5
  1593.2 98.6 %all-gather.12.cloned.1.call-start = ((), (), s32[]{:S(2)}) async-start(), calls=%async_computation.15 | async-start | bytes 1081344 | tf_op jit(solution)/shard_map/all_gather | solution.py:52
Sparse Core Ops, SparseCore 0:
  10.7 36.9 all-gather.5
  51.0 53.8 all-reduce.6
  107.9 34.1 all-gather.7
  145.7 53.8 all-reduce.8
  202.0 129.7 all-reduce.10
  945.2 234.8 all-reduce.12
  1248.5 29.0 reduce-scatter.9
  1323.1 36.9 reduce-scatter.11
  1405.8 36.9 reduce-scatter.13
  1489.1 37.2 reduce-scatter.15
  1530.5 59.1 all-gather.9
  1593.4 35.6 reduce-scatter.17
  1632.7 59.1 all-gather.11
where the time goes:
time: 1700 us
  waiting for transfers between devices  844 us (50%)
  blocking collectives  799 us (47%)
  matrix products  23 us (1%)
    psum x2, blocking collectives, blocks_layout(): lax.psum(jnp.einsum('mn,mar->nar', spot_table, upward), ('col', 'gz'))  445 us
    psum x1, waiting for transfers between devices, blocks_layout(): lax.psum(jnp.einsum('mn,mar->nar', spot_table, upward), ('col', 'gz'))  234 us
    all_gather x4, blocking collectives, broadcast_rows(): return lax.all_gather(values, 'row', axis=1, tiled=True)  183 us
    all_gather x4, blocking collectives, back_solve(): lax.all_gather(own_share.astype(jnp.bfloat16), ('row', 'col'), axis=1, ti...  171 us
    psum x1, waiting for transfers between devices, blocks_layout(): lax.psum(spread_all.astype(jnp.bfloat16), 'gz').astype(jnp.float32)  130 us
    all_gather x2, waiting for transfers between devices, back_solve(): lax.all_gather(own_share.astype(jnp.bfloat16), ('row', 'col'), axis=1, ti...  122 us
    reduce_scatter x3, waiting for transfers between devices, back_solve(): lax.psum_scatter(partial_value.astype(jnp.bfloat16), 'row', scatter_dimen...  103 us
    all_gather x2, waiting for transfers between devices, broadcast_rows(): return lax.all_gather(values, 'row', axis=1, tiled=True)  74 us
  transfers between devices with their start and end apart: 13, of which 13 were waited for; matrix products, arithmetic and copies ran while one was open for 0% of the time, Pallas kernels for 0%

commit v1 on v0

v1 whole, which is shorter than its diff:
```python
import functools

import jax
import jax.numpy as jnp
from jax import lax
from jax.experimental import pallas as pl
from jax.experimental.pallas import tpu as pltpu
from jax.sharding import PartitionSpec as P

F32 = jnp.float32
BF16 = jnp.bfloat16
MESH = pl.DeviceIdType.MESH
ROWS, COLS, LAYERS = 8, 4, 16
NPL, LOC, TOPL = 4, 8, 4
W, R = 256, 512
SLAB, KCH = W // ROWS, W // COLS
CG = R // COLS
CP = CG // ROWS
L_PAIRS = ((0, 1), (0, 2), (0, 3), (1, 2), (1, 3), (2, 3))
Z_BASE = (0, 4, 7, 9)


def nt(a, b):
    return lax.dot_general(a, b, (((1,), (1,)), ((), ())), preferred_element_type=F32)


def mm(a, b):
    return jnp.dot(a, b, preferred_element_type=F32)


def aligned(value, size):
    return pl.ds(pl.multiple_of(value * size, size), size)


def kernel(
    parent, l_tree, l_path, l_top, u_tree, u_path, u_top, linv_local, linv_top, uinv_local,
    uinv_top, rhs_local, rhs_top, x_local, x_path,
    st_ltree, st_lpath, st_ltop, st_utree, st_upath, st_utop, uinv_own, rhs2_own, st_rt,
    x1, linv, lt, lp, ltp1, ltp, linvt, uinvt, uinv2, up, us, ut,
    y, ylow, s2f, tt, rv, rt, rr, zs, zr, xp, sb2, x2low, sb1, out_l, out_p,
    lsem, ssem, rsem,
):
    r = lax.axis_index("row")
    c = lax.axis_index("col")
    g = lax.axis_index("gz")
    counters = {"l": 0, "s": 0, "r": 0}
    pending_sends = []

    def take(kind, count=1):
        first = counters[kind]
        counters[kind] += count
        return first

    def local(src, dst):
        copy = pltpu.make_async_copy(src, dst, lsem.at[take("l")])
        copy.start()
        return copy

    def remote(src, dst, slot, target):
        copy = pltpu.make_async_remote_copy(
            src_ref=src, dst_ref=dst, send_sem=ssem.at[take("s")], recv_sem=rsem.at[slot],
            device_id=target, device_id_type=MESH,
        )
        copy.start()
        pending_sends.append(copy)

    def await_slot(dst, slot):
        pltpu.make_async_remote_copy(
            src_ref=dst, dst_ref=dst, send_sem=ssem.at[0], recv_sem=rsem.at[slot],
            device_id={"row": r}, device_id_type=MESH,
        ).wait_recv()

    def spread(axis, src_of, dst_of):
        me, size = (r, ROWS) if axis == "row" else (c, COLS)
        base = take("r", size)
        for step in range(1, size):
            peer = lax.rem(me + step, size)
            remote(src_of(peer), dst_of(me), base + step, {axis: peer})

        def wait():
            for step in range(1, size):
                await_slot(dst_of(lax.rem(me + size - step, size)), base + step)

        return wait

    anc = [LAYERS - (LAYERS >> a) + g // 2 ** (a + 1) for a in range(TOPL)]
    my_rows = aligned(r, SLAB)
    my_k = aligned(c, KCH)
    my_cols = aligned(c, CG)

    barrier = pltpu.get_barrier_semaphore()
    for step in range(1, ROWS):
        pl.semaphore_signal(barrier, inc=1, device_id={"row": lax.rem(r + step, ROWS)}, device_id_type=MESH)
    for step in range(1, COLS):
        pl.semaphore_signal(barrier, inc=1, device_id={"col": lax.rem(c + step, COLS)}, device_id_type=MESH)
    partners = []
    for a in range(TOPL):
        span = 2**a
        partners.append(g + span - 2 * span * lax.rem(g // span, 2))
        pl.semaphore_signal(barrier, inc=1, device_id={"gz": partners[a]}, device_id_type=MESH)

    c_ltree = local(l_tree, st_ltree)
    c_lpath = local(l_path, st_lpath)
    c_ltop = [local(l_top.at[anc[a]], st_ltop.at[a]) for a in range(3)]
    c_rt = [local(rhs_top.at[anc[a], :, my_cols], st_rt.at[a]) for a in range(TOPL)]
    c_x1 = local(rhs_local.at[pl.ds(0, NPL), :, my_cols], x1.at[:, my_rows, :])
    c_li1 = local(linv_local.at[pl.ds(0, NPL)], linv.at[pl.ds(0, NPL), my_k, :])
    c_li2 = local(linv_local.at[pl.ds(NPL, NPL)], linv.at[pl.ds(NPL, NPL), my_k, :])
    c_lit = [local(linv_top.at[anc[a]], linvt.at[a, my_k, :]) for a in range(TOPL)]
    c_rhs2 = local(rhs_local.at[pl.ds(NPL, NPL), :, my_cols], rhs2_own)
    c_utree = local(u_tree, st_utree)
    c_upath = local(u_path, st_upath)
    c_utop = [local(u_top.at[anc[a]], st_utop.at[a]) for a in range(3)]
    c_uiown = local(uinv_local, uinv_own)
    c_ui2 = local(uinv_local.at[pl.ds(NPL, NPL)], uinv2.at[:, my_rows, :])
    c_uit = [local(uinv_top.at[anc[a]], uinvt.at[a, my_rows, :]) for a in range(TOPL)]

    pl.semaphore_wait(barrier, ROWS - 1 + COLS - 1 + TOPL)

    w_x1 = spread(
        "row", lambda peer: rhs_local.at[pl.ds(0, NPL), :, my_cols],
        lambda me: x1.at[:, aligned(me, SLAB), :],
    )
    w_li1 = spread(
        "col", lambda peer: linv_local.at[pl.ds(0, NPL)],
        lambda me: linv.at[pl.ds(0, NPL), aligned(me, KCH), :],
    )
    odd = lax.rem(c, 2)

    def shifted(block):
        blank = jnp.zeros_like(block)
        low = jnp.concatenate([block, blank], axis=-1)
        high = jnp.concatenate([blank, block], axis=-1)
        return jnp.where(odd == 0, low, high)

    c_ltree.wait()
    for j in range(NPL):
        lt[c, j] = shifted(st_ltree[j])
    w_lt = spread("col", lambda peer: lt.at[c], lambda me: lt.at[me])
    w_li2 = spread(
        "col", lambda peer: linv_local.at[pl.ds(NPL, NPL)],
        lambda me: linv.at[pl.ds(NPL, NPL), aligned(me, KCH), :],
    )
    c_lpath.wait()
    for m in range(TOPL):
        lp[c, pl.ds(m * SLAB, SLAB), :] = jnp.concatenate([st_lpath[k, m] for k in range(LOC)], axis=-1)
    w_lp = spread("col", lambda peer: lp.at[c], lambda me: lp.at[me])
    for copy in c_ltop:
        copy.wait()
    for b, (a, m) in enumerate(L_PAIRS):
        ltp1[c, b] = shifted(st_ltop[a, m])
    w_ltp1 = spread("col", lambda peer: ltp1.at[c], lambda me: ltp1.at[me])
    for copy in c_lit:
        copy.wait()
    w_lit = spread("col", lambda peer: linvt.at[:, my_k, :], lambda me: linvt.at[:, aligned(me, KCH), :])

    eye = (
        lax.broadcasted_iota(jnp.int32, (CG, CG), 0) == lax.broadcasted_iota(jnp.int32, (CG, CG), 1)
    ).astype(F32).astype(BF16)
    for copy in c_rt:
        copy.wait()
    rt[...] = nt(eye, st_rt[...].reshape(TOPL * SLAB, CG)).astype(BF16)
    w_rr = spread("row", lambda peer: rt.at[aligned(peer, CP), :], lambda me: rr.at[me])
    rr[r] = rt[aligned(r, CP), :]

    eye_k = eye[0:KCH, 0:KCH]

    def packed(stack):
        return nt(eye_k, stack).astype(BF16)

    c_upath.wait()
    for k in range(LOC):
        up[k, my_k, :] = packed(st_upath[k].reshape(CG, KCH))
    c_utree.wait()
    up[LOC, my_k, :] = packed(st_utree[...].reshape(CG, KCH))
    for copy in c_utop:
        copy.wait()
    up[LOC + 1, my_k, :] = packed(jnp.concatenate([st_utop[2, 3], st_utop[0, 1], st_utop[0, 2], st_utop[0, 3]], axis=0))
    up[LOC + 2, my_k, :] = packed(st_utop[1].reshape(CG, KCH))

    c_x1.wait()
    c_li1.wait()
    w_x1()
    w_li1()
    for j in range(NPL):
        solved = mm(linv[j], x1[j])
        y[j] = solved
        ylow[j] = solved.astype(BF16)
    w_lt()
    terms = []
    for j in range(NPL):
        term = mm(lt[0, j] + lt[1, j], ylow[j, 0:CG, :]) + mm(lt[2, j] + lt[3, j], ylow[j, CG:W, :])
        terms.append(term)
    c_rhs2.wait()
    for i in range(NPL):
        value = rhs2_own[i].astype(F32)
        for j in range(NPL):
            value = value - jnp.where(parent[j] == i, 1.0, 0.0).astype(F32) * terms[j]
        s2f[i, my_rows, :] = value.astype(BF16)
    w_s2 = spread("row", lambda peer: s2f.at[:, my_rows, :], lambda me: s2f.at[:, aligned(me, SLAB), :])

    w_up = spread("col", lambda peer: up.at[:, my_k, :], lambda me: up.at[:, aligned(me, KCH), :])
    w_ltp1()
    for b in range(len(L_PAIRS)):
        ltp[b, my_rows, :] = jnp.concatenate([ltp1[0, b] + ltp1[1, b], ltp1[2, b] + ltp1[3, b]], axis=-1)
    w_ltp = spread("row", lambda peer: ltp.at[:, my_rows, :], lambda me: ltp.at[:, aligned(me, SLAB), :])
    for copy in c_uit:
        copy.wait()

    w_lp()
    toward = jnp.zeros((TOPL * SLAB, CG), F32)
    for q in range(COLS):
        block = ylow[0:NPL, q * KCH:(q + 1) * KCH, :].reshape(NPL * KCH, CG)
        toward = toward + mm(lp[q, :, 0:NPL * KCH], block)

    c_li2.wait()
    w_li2()
    w_s2()
    for i in range(NPL):
        solved = mm(linv[NPL + i], s2f[i])
        y[NPL + i] = solved
        ylow[NPL + i] = solved.astype(BF16)
    for q in range(COLS):
        block = ylow[NPL:LOC, q * KCH:(q + 1) * KCH, :].reshape(NPL * KCH, CG)
        toward = toward + mm(lp[q, :, NPL * KCH:LOC * KCH], block)
    tt[...] = nt(eye, toward.astype(BF16)).astype(BF16)
    w_rv = spread("row", lambda peer: tt.at[aligned(peer, CP), :], lambda me: rv.at[me])
    rv[r] = tt[aligned(r, CP), :]

    w_uit = spread("row", lambda peer: uinvt.at[:, my_rows, :], lambda me: uinvt.at[:, aligned(me, SLAB), :])

    slot_of_lane = lax.broadcasted_iota(jnp.int32, (CP, CG), 1) // SLAB

    def by_level(tiles, m):
        halves = []
        for q in range(2):
            total = None
            for s in range(4):
                piece = tiles[4 * q + s]
                if s != m:
                    piece = pltpu.roll(piece, (s - m) * SLAB % CG, 1)
                total = piece if total is None else jnp.where(slot_of_lane == s, piece, total)
            halves.append(total)
        return jnp.concatenate(halves, axis=-1)

    w_rr()
    rr_tiles = [rr[q].astype(F32) for q in range(ROWS)]
    top_rhs = [by_level(rr_tiles, m) for m in range(TOPL)]
    w_rv()
    rv_tiles = [rv[q].astype(F32) for q in range(ROWS)]
    pend = [by_level(rv_tiles, m) for m in range(TOPL)]

    top_y = []
    w_us = w_ut = None
    for a in range(TOPL):
        count = TOPL - a
        base = Z_BASE[a]
        for m in range(a, TOPL):
            zs[base + m - a] = pend[m].astype(BF16)
        slot = take("r")
        remote(zs.at[pl.ds(base, count)], zr.at[pl.ds(base, count)], slot, {"gz": partners[a]})
        if a == 0:
            c_ui2.wait()
            w_ui2 = spread("row", lambda peer: uinv2.at[:, my_rows, :], lambda me: uinv2.at[:, aligned(me, SLAB), :])
            w_up()
            u_lanes = pl.ds(pl.multiple_of(r * CG, CG), CG)
            w_ut = spread(
                "row", lambda peer: up.at[pl.ds(LOC + 1, 2)],
                lambda me: ut.at[:, :, pl.ds(pl.multiple_of(me * CG, CG), CG)],
            )
            w_us = spread(
                "row", lambda peer: up.at[pl.ds(0, LOC + 1), aligned(peer, SLAB), :],
                lambda me: us.at[:, :, pl.ds(pl.multiple_of(me * CG, CG), CG)],
            )
            c_ut = local(up.at[pl.ds(LOC + 1, 2)], ut.at[:, :, u_lanes])
            c_us = local(up.at[pl.ds(0, LOC + 1), my_rows, :], us.at[:, :, u_lanes])
            w_lit()
            w_ltp()
        await_slot(zr.at[pl.ds(base, count)], slot)
        for m in range(a, TOPL):
            pend[m] = pend[m] + zr[base + m - a].astype(F32)
        solved = nt((top_rhs[a] - pend[a]).astype(BF16), linvt[a])
        top_y.append(solved)
        low = solved.astype(BF16)
        for b, (source, m) in enumerate(L_PAIRS):
            if source == a:
                pend[m] = pend[m] + nt(low, ltp[b])

    c_ut.wait()
    w_ut()
    w_uit()
    tiles = [jnp.zeros((CP, CG), F32) for _ in range(ROWS)]
    for a in reversed(range(TOPL)):
        value = top_y[a]
        if a < TOPL - 1:
            if a == 2:
                known = [pltpu.roll(tile, SLAB, 1) for tile in tiles]
            else:
                known = tiles
            above = jnp.concatenate(known, axis=-1).astype(BF16)
            value = value - nt(above, ut[0 if a != 1 else 1])
        solved = nt(value.astype(BF16), uinvt[a])
        for q in range(2):
            half = solved[:, q * CG:(q + 1) * CG]
            for s in range(4):
                piece = half if a == s else pltpu.roll(half, (a - s) * SLAB % CG, 1)
                tiles[4 * q + s] = jnp.where(slot_of_lane == a, piece, tiles[4 * q + s])
    my_cp = aligned(r, CP)
    xp[my_cp, :] = jnp.concatenate(tiles, axis=-1).astype(BF16)
    w_xp = spread("row", lambda peer: xp.at[my_cp, :], lambda me: xp.at[aligned(me, CP), :])

    c_us.wait()
    w_us()
    w_xp()
    path = xp[...]
    path_term2 = nt(us[NPL:LOC].reshape(NPL * SLAB, ROWS * CG), path)
    for i in range(NPL):
        value = y[NPL + i, my_rows, :] - path_term2[i * SLAB:(i + 1) * SLAB, :]
        sb2[i, my_rows, :] = value.astype(BF16)
    w_sb2 = spread("row", lambda peer: sb2.at[:, my_rows, :], lambda me: sb2.at[:, aligned(me, SLAB), :])
    path_term1 = nt(us[0:NPL].reshape(NPL * SLAB, ROWS * CG), path)
    own_path = nt(eye, xp[:, pl.ds(pl.multiple_of(r * CG, CG), CG)])
    for m in range(TOPL):
        out_p[m] = own_path[m * SLAB:(m + 1) * SLAB, :]
    piece_rows = SLAB // COLS

    def out_rows(peer):
        return pl.ds(pl.multiple_of(peer * piece_rows, piece_rows), piece_rows)

    w_outp = spread(
        "col", lambda peer: out_p.at[:, out_rows(peer), :],
        lambda me: x_path.at[0, :, :, pl.ds(pl.multiple_of(me * CG, CG), CG)],
    )
    c_outp = local(out_p.at[:, out_rows(c), :], x_path.at[0, :, :, my_cols])
    lane_slot = lax.rem(lax.broadcasted_iota(jnp.int32, (SLAB, ROWS * CG), 1) // SLAB, NPL)
    tree_piece = us[LOC]
    tree_blocks = [jnp.where(lane_slot == j, tree_piece, jnp.zeros_like(tree_piece)) for j in range(NPL)]
    tree_weights = jnp.concatenate(tree_blocks, axis=0)

    w_ui2()
    c_uiown.wait()
    w_sb2()
    for i in range(NPL):
        x2low[i] = mm(uinv2[i], sb2[i]).astype(BF16)
    parent_x = [x2low[parent[j]].reshape(ROWS, 1, SLAB, CG) for j in range(NPL)]
    stacked = jnp.concatenate(parent_x, axis=1).reshape(ROWS * NPL * SLAB, CG)
    tree_term = mm(tree_weights, stacked)
    for j in range(NPL):
        rows = slice(j * SLAB, (j + 1) * SLAB)
        value = y[j, my_rows, :] - path_term1[rows, :] - tree_term[rows, :]
        sb1[j, my_rows, :] = value.astype(BF16)
    w_sb1 = spread("row", lambda peer: sb1.at[:, my_rows, :], lambda me: sb1.at[:, aligned(me, SLAB), :])
    for i in range(NPL):
        out_l[NPL + i] = mm(uinv_own[NPL + i], sb2[i])

    def send_out(first):
        part = pl.ds(first, NPL)
        wait = spread(
            "col", lambda peer: out_l.at[part, out_rows(peer), :],
            lambda me: x_local.at[part, :, pl.ds(pl.multiple_of(me * CG, CG), CG)],
        )
        return wait, local(out_l.at[part, out_rows(c), :], x_local.at[part, :, my_cols])

    w_out2, c_out2 = send_out(NPL)
    w_sb1()
    for j in range(NPL):
        out_l[j] = mm(uinv_own[j], sb1[j])
    w_out1, c_out1 = send_out(0)
    w_outp()
    w_out2()
    w_out1()
    for copy in (c_outp, c_out2, c_out1):
        copy.wait()
    for copy in pending_sends:
        copy.wait_send()


def per_device(*arrays):
    arrays = list(arrays)
    for index in (4, 5, 6):
        arrays[index] = jnp.swapaxes(arrays[index], -1, -2)
    any_space = pl.BlockSpec(memory_space=pl.ANY)
    vmem = pltpu.VMEM
    scratch = [
        vmem((NPL, SLAB, KCH), BF16),
        vmem((LOC, TOPL, SLAB, KCH), BF16),
        vmem((3, TOPL, SLAB, KCH), BF16),
        vmem((NPL, SLAB, KCH), BF16),
        vmem((LOC, TOPL, SLAB, KCH), BF16),
        vmem((3, TOPL, SLAB, KCH), BF16),
        vmem((LOC, SLAB, W), BF16),
        vmem((NPL, SLAB, CG), BF16),
        vmem((TOPL, SLAB, CG), BF16),
        vmem((NPL, W, CG), BF16),
        vmem((LOC, W, W), BF16),
        vmem((COLS, NPL, SLAB, CG), BF16),
        vmem((COLS, TOPL * SLAB, LOC * KCH), BF16),
        vmem((COLS, 6, SLAB, CG), BF16),
        vmem((6, W, W), BF16),
        vmem((TOPL, W, W), BF16),
        vmem((TOPL, W, W), BF16),
        vmem((NPL, W, W), BF16),
        vmem((LOC + 3, W, CG), BF16),
        vmem((LOC + 1, SLAB, ROWS * CG), BF16),
        vmem((2, W, ROWS * CG), BF16),
        vmem((LOC, W, CG), F32),
        vmem((LOC, W, CG), BF16),
        vmem((NPL, W, CG), BF16),
        vmem((CG, TOPL * SLAB), BF16),
        vmem((ROWS, CP, CG), BF16),
        vmem((CG, TOPL * SLAB), BF16),
        vmem((ROWS, CP, CG), BF16),
        vmem((10, CP, W), BF16),
        vmem((10, CP, W), BF16),
        vmem((CG, ROWS * CG), BF16),
        vmem((NPL, W, CG), BF16),
        vmem((NPL, W, CG), BF16),
        vmem((NPL, W, CG), BF16),
        vmem((LOC, SLAB, CG), F32),
        vmem((TOPL, SLAB, CG), F32),
        pltpu.SemaphoreType.DMA((48,)),
        pltpu.SemaphoreType.DMA((160,)),
        pltpu.SemaphoreType.DMA((160,)),
    ]
    return pl.pallas_call(
        kernel,
        out_shape=(
            jax.ShapeDtypeStruct((LOC, SLAB // COLS, R), F32),
            jax.ShapeDtypeStruct((1, TOPL, SLAB // COLS, R), F32),
        ),
        in_specs=[pl.BlockSpec(memory_space=pltpu.SMEM)] + [any_space] * 12,
        out_specs=(any_space, any_space),
        scratch_shapes=scratch,
        compiler_params=pltpu.CompilerParams(
            collective_id=0, has_side_effects=True, vmem_limit_bytes=60 * 1024 * 1024
        ),
    )(*arrays)


def solution(mesh):
    placed = (
        P("gz"),
        P("gz", "row", "col"),
        P("gz", None, "row", "col"),
        P(None, None, "row", "col"),
        P("gz", "col", "row"),
        P("gz", None, "col", "row"),
        P(None, None, "col", "row"),
        P("gz", "col", None),
        P(None, "col", None),
        P("gz", "row", None),
        P(None, "row", None),
        P("gz", "row", None),
        P(None, "row", None),
    )
    return jax.shard_map(
        per_device,
        mesh=mesh,
        in_specs=placed,
        out_specs=(P("gz", ("row", "col"), None), P("gz", None, ("row", "col"), None)),
        check_vma=False,
    )
```

time: 1700 us -> 104 us (0.06)
  waiting for transfers between devices: 844 us -> 0 us
  blocking collectives: 799 us -> 0 us
  Pallas kernels: 0 us -> 101 us
  matrix products: 23 us -> 0 us
    psum x4 -> x0, waiting for transfers between devices: 471 us -> none  [the longest x1 234 us: blocks_layout(): lax.psum(jnp.einsum('mn,mar->nar', spot_table, upward), ('col', 'gz'))]
    psum x2 -> x0, blocking collectives: 445 us -> none  [blocks_layout(): lax.psum(jnp.einsum('mn,mar->nar', spot_table, upward), ('col', 'gz'))]
    all_gather x8 -> x0, blocking collectives: 353 us -> none  [the longest x4 183 us: broadcast_rows(): return lax.all_gather(values, 'row', axis=1, tiled=True)]
    all_gather x4 -> x0, waiting for transfers between devices: 196 us -> none  [the longest x2 122 us: back_solve(): lax.all_gather(own_share.astype(jnp.bfloat16), ('row', 'col'), axis=1, ti...]
    reduce_scatter x3 -> x0, waiting for transfers between devices: 103 us -> none  [back_solve(): lax.psum_scatter(partial_value.astype(jnp.bfloat16), 'row', scatter_dimen...]
    pallas_call x0 -> x1, Pallas kernels: none -> 101 us  [per_device(): pl.pallas_call(kernel, out_shape=(jax.ShapeDtypeStruct((LOC, SLAB // COLS...]
    unnamed x15 -> x0, waiting for transfers between devices: 73.3 us -> none
    dot_general x30 -> x0, matrix products: 23 us -> none  [the longest x3 4.63 us: blocks_layout(): jnp.einsum('mab,mbr->ar', blocks, above, preferred_element_type=jnp.float32)]
  transfers between devices with their start and end apart: 13 -> 0, of which waited for: 13 -> 0; matrix products, arithmetic and copies ran while one was open for 0% -> 0% of each run, Pallas kernels for 0% -> 0%
where the time goes in v1:
time: 104 us
  Pallas kernels  101 us (97%)
  local copies, waits for them, and re-layouts  2.23 us (2%)
    pallas_call x1, Pallas kernels, per_device(): pl.pallas_call(kernel, out_shape=(jax.ShapeDtypeStruct((LOC, SLAB // COLS...  101 us
    unnamed x4, local copies, waits for them, and re-layouts  2.23 us

profile of v1, /device:TPU:1, one launch (start us, length us, event | category | flops | bytes accessed | tf_op | source)
XLA Modules:
  0.0 104.2 jit_solution(2579945246513963109)
XLA Ops:
  0.6 101.3 %shard_map.140 = (f32[8,8,512]{2,1,0:T(8,128)}, f32[1,4,8,512]{3,2,1,0:T(8,128)}) custom-call(s32[4]{0:T(128)} %parent.1, bf16[4,32,64]{2,1,0:T(8,128)(2,1)} %l_tree.1, bf16[8,4,32,64]{3,2,1,0:T(8,128)(2,1)} %l_path.1, bf16[15,4,32,64]{3,2,1,0:T(8,128)(2,1)} %l_top.1, bf16[4,32,64]{2,1,0:T(8,128)(2,1)} %bitcast.5, bf16[8,4,32,64]{3,2,1,0:T(8,128)(2,1)} %bitcast.4, ...), custom_call_target="tpu_custom_call" | custom-call | tf_op jit(solution)/shard_map/pallas_call | solution.py:425
  101.9 0.0 copy-start
  102.0 1.6 %copy.17 = f32[8,8,512]{2,1,0:T(8,128)} copy(f32[8,8,512]{2,1,0:T(8,128)} %get-tuple-element.4) | data formatting | bytes 262144
  103.6 0.0 copy-done
  103.6 0.6 copy.18
Async XLA Ops:
  101.9 1.6 %copy-start = (f32[1,4,8,512]{3,2,1,0:T(8,128)S(1)}, f32[1,4,8,512]{3,2,1,0:T(8,128)}, u32[]{:S(2)}) copy-start(f32[1,4,8,512]{3,2,1,0:T(8,128)} %get-tuple-element.5) | copy-start | bytes 196612

commit v2 on v1

--- a/solution.py
+++ b/solution.py
@@ -36,13 +36,15 @@
     parent, l_tree, l_path, l_top, u_tree, u_path, u_top, linv_local, linv_top, uinv_local,
     uinv_top, rhs_local, rhs_top, x_local, x_path,
     st_ltree, st_lpath, st_ltop, st_utree, st_upath, st_utop, uinv_own, rhs2_own, st_rt,
-    x1, linv, lt, lp, ltp1, ltp, linvt, uinvt, uinv2, up, us, ut,
+    x1, linv, lt, lp, ltp1, ltp, linvt, uinvt, uinv2, up, us, utp, ut, tree_w,
     y, ylow, s2f, tt, rv, rt, rr, zs, zr, xp, sb2, x2low, sb1, out_l, out_p,
     lsem, ssem, rsem,
 ):
     r = lax.axis_index("row")
     c = lax.axis_index("col")
     g = lax.axis_index("gz")
+    chip, core = r // 2, lax.rem(r, 2)
+    sibling = chip * 2 + 1 - core
     counters = {"l": 0, "s": 0, "r": 0}
     pending_sends = []
 
@@ -83,47 +85,104 @@
 
         return wait
 
+    def row_of(other_chip, other_core):
+        return lax.rem(other_chip + 4, 4) * 2 + other_core
+
+    def spread_row_shared(src, dst_of):
+        base = take("r", 8)
+        for step in range(1, 4):
+            remote(src, dst_of(r), base + step, {"row": row_of(chip + step, core)})
+        remote(src, dst_of(r), base, {"row": sibling})
+
+        def forward():
+            for step in range(1, 4):
+                place = dst_of(row_of(chip - step, core))
+                await_slot(place, base + step)
+                remote(place, place, base + 4 + step, {"row": sibling})
+
+        def wait():
+            await_slot(dst_of(sibling), base)
+            for step in range(1, 4):
+                await_slot(dst_of(row_of(chip - step, 1 - core)), base + 4 + step)
+
+        return forward, wait
+
+    def spread_col_shared(src, dst_of):
+        base = take("r", 8)
+        for step in range(1, COLS):
+            remote(src, dst_of(c, core), base + step, {"col": lax.rem(c + step, COLS)})
+
+        def forward():
+            for step in range(1, COLS):
+                place = dst_of(lax.rem(c + COLS - step, COLS), core)
+                await_slot(place, base + step)
+                remote(place, place, base + 4 + step, {"row": sibling})
+
+        def wait():
+            for step in range(1, COLS):
+                await_slot(dst_of(lax.rem(c + COLS - step, COLS), 1 - core), base + 4 + step)
+
+        return forward, wait
+
     anc = [LAYERS - (LAYERS >> a) + g // 2 ** (a + 1) for a in range(TOPL)]
     my_rows = aligned(r, SLAB)
     my_k = aligned(c, KCH)
     my_cols = aligned(c, CG)
+    half_src = aligned(core, SLAB)
+
+    def half_rows(owner, half):
+        return aligned(owner * 2 + half, SLAB)
+
+    def lanes_of(owner):
+        return pl.ds(pl.multiple_of(owner * CG, CG), CG)
 
     barrier = pltpu.get_barrier_semaphore()
-    for step in range(1, ROWS):
-        pl.semaphore_signal(barrier, inc=1, device_id={"row": lax.rem(r + step, ROWS)}, device_id_type=MESH)
-    for step in range(1, COLS):
-        pl.semaphore_signal(barrier, inc=1, device_id={"col": lax.rem(c + step, COLS)}, device_id_type=MESH)
+
+    def greet(target):
+        pl.semaphore_signal(barrier, inc=1, device_id=target, device_id_type=MESH)
+
     partners = []
-    for a in range(TOPL):
+    for a in range(TOPL - 1):
         span = 2**a
         partners.append(g + span - 2 * span * lax.rem(g // span, 2))
-        pl.semaphore_signal(barrier, inc=1, device_id={"gz": partners[a]}, device_id_type=MESH)
-
+    quarter = g // 4
+    source = jnp.where(quarter == 0, 15, jnp.where(quarter == 1, 8, jnp.where(quarter == 2, 7, 0)))
+    edge = jnp.logical_or(jnp.logical_or(g == 0, g == 7), jnp.logical_or(g == 8, g == 15))
+    first_target = jnp.where(g == 0, 12, jnp.where(g == 7, 8, jnp.where(g == 8, 4, 0)))
+    for step in range(1, ROWS):
+        greet({"row": lax.rem(r + step, ROWS)})
+    for step in range(ROWS):
+        greet({"row": lax.rem(r + step, ROWS), "gz": partners[0]})
+    for step in range(1, COLS):
+        greet({"col": lax.rem(c + step, COLS)})
+    greet({"gz": partners[1]})
+    greet({"gz": partners[2]})
+    greet({"gz": source})
+
+    c_x1 = local(rhs_local.at[pl.ds(0, NPL), :, my_cols], x1.at[:, my_rows, :])
+    c_li1 = local(linv_local.at[pl.ds(0, NPL)], linv.at[pl.ds(0, NPL), my_k, :])
     c_ltree = local(l_tree, st_ltree)
     c_lpath = local(l_path, st_lpath)
     c_ltop = [local(l_top.at[anc[a]], st_ltop.at[a]) for a in range(3)]
+    c_lit = [local(linv_top.at[anc[a]], linvt.at[a, my_k, :]) for a in range(TOPL)]
+    c_uit = [local(uinv_top.at[anc[a]], uinvt.at[a, my_rows, :]) for a in range(TOPL)]
     c_rt = [local(rhs_top.at[anc[a], :, my_cols], st_rt.at[a]) for a in range(TOPL)]
-    c_x1 = local(rhs_local.at[pl.ds(0, NPL), :, my_cols], x1.at[:, my_rows, :])
-    c_li1 = local(linv_local.at[pl.ds(0, NPL)], linv.at[pl.ds(0, NPL), my_k, :])
     c_li2 = local(linv_local.at[pl.ds(NPL, NPL)], linv.at[pl.ds(NPL, NPL), my_k, :])
-    c_lit = [local(linv_top.at[anc[a]], linvt.at[a, my_k, :]) for a in range(TOPL)]
     c_rhs2 = local(rhs_local.at[pl.ds(NPL, NPL), :, my_cols], rhs2_own)
+    c_utop = [local(u_top.at[anc[a]], st_utop.at[a]) for a in range(3)]
     c_utree = local(u_tree, st_utree)
     c_upath = local(u_path, st_upath)
-    c_utop = [local(u_top.at[anc[a]], st_utop.at[a]) for a in range(3)]
+    c_ui2 = local(uinv_local.at[pl.ds(NPL, NPL)], uinv2.at[:, my_rows, :])
     c_uiown = local(uinv_local, uinv_own)
-    c_ui2 = local(uinv_local.at[pl.ds(NPL, NPL)], uinv2.at[:, my_rows, :])
-    c_uit = [local(uinv_top.at[anc[a]], uinvt.at[a, my_rows, :]) for a in range(TOPL)]
-
-    pl.semaphore_wait(barrier, ROWS - 1 + COLS - 1 + TOPL)
+
+    pl.semaphore_wait(barrier, ROWS - 1 + ROWS + COLS - 1 + 2 + jnp.where(edge, 4, 0))
 
     w_x1 = spread(
         "row", lambda peer: rhs_local.at[pl.ds(0, NPL), :, my_cols],
         lambda me: x1.at[:, aligned(me, SLAB), :],
     )
-    w_li1 = spread(
-        "col", lambda peer: linv_local.at[pl.ds(0, NPL)],
-        lambda me: linv.at[pl.ds(0, NPL), aligned(me, KCH), :],
+    f_li1, w_li1 = spread_col_shared(
+        linv_local.at[pl.ds(0, NPL), half_src], lambda o, h: linv.at[pl.ds(0, NPL), half_rows(o, h), :]
     )
     odd = lax.rem(c, 2)
 
@@ -137,9 +196,8 @@
     for j in range(NPL):
         lt[c, j] = shifted(st_ltree[j])
     w_lt = spread("col", lambda peer: lt.at[c], lambda me: lt.at[me])
-    w_li2 = spread(
-        "col", lambda peer: linv_local.at[pl.ds(NPL, NPL)],
-        lambda me: linv.at[pl.ds(NPL, NPL), aligned(me, KCH), :],
+    f_li2, w_li2 = spread_col_shared(
+        linv_local.at[pl.ds(NPL, NPL), half_src], lambda o, h: linv.at[pl.ds(NPL, NPL), half_rows(o, h), :]
     )
     c_lpath.wait()
     for m in range(TOPL):
@@ -152,7 +210,12 @@
     w_ltp1 = spread("col", lambda peer: ltp1.at[c], lambda me: ltp1.at[me])
     for copy in c_lit:
         copy.wait()
-    w_lit = spread("col", lambda peer: linvt.at[:, my_k, :], lambda me: linvt.at[:, aligned(me, KCH), :])
+    f_lit, w_lit = spread_col_shared(
+        linvt.at[:, half_rows(c, core), :], lambda o, h: linvt.at[:, half_rows(o, h), :]
+    )
+    for copy in c_uit:
+        copy.wait()
+    f_uit, w_uit = spread_row_shared(uinvt.at[:, my_rows, :], lambda me: uinvt.at[:, aligned(me, SLAB), :])
 
     eye = (
         lax.broadcasted_iota(jnp.int32, (CG, CG), 0) == lax.broadcasted_iota(jnp.int32, (CG, CG), 1)
@@ -162,24 +225,28 @@
     rt[...] = nt(eye, st_rt[...].reshape(TOPL * SLAB, CG)).astype(BF16)
     w_rr = spread("row", lambda peer: rt.at[aligned(peer, CP), :], lambda me: rr.at[me])
     rr[r] = rt[aligned(r, CP), :]
+    c_ui2.wait()
+    f_ui2, w_ui2 = spread_row_shared(uinv2.at[:, my_rows, :], lambda me: uinv2.at[:, aligned(me, SLAB), :])
 
     eye_k = eye[0:KCH, 0:KCH]
 
     def packed(stack):
         return nt(eye_k, stack).astype(BF16)
 
+    for copy in c_utop:
+        copy.wait()
+    utp[0, my_k, :] = packed(jnp.concatenate([st_utop[2, 3], st_utop[0, 1], st_utop[0, 2], st_utop[0, 3]], axis=0))
+    utp[1, my_k, :] = packed(st_utop[1].reshape(CG, KCH))
+    c_utree.wait()
+    utp[2, my_k, :] = packed(st_utree[...].reshape(CG, KCH))
+    w_utp = spread("col", lambda peer: utp.at[:, my_k, :], lambda me: utp.at[:, aligned(me, KCH), :])
     c_upath.wait()
     for k in range(LOC):
         up[k, my_k, :] = packed(st_upath[k].reshape(CG, KCH))
-    c_utree.wait()
-    up[LOC, my_k, :] = packed(st_utree[...].reshape(CG, KCH))
-    for copy in c_utop:
-        copy.wait()
-    up[LOC + 1, my_k, :] = packed(jnp.concatenate([st_utop[2, 3], st_utop[0, 1], st_utop[0, 2], st_utop[0, 3]], axis=0))
-    up[LOC + 2, my_k, :] = packed(st_utop[1].reshape(CG, KCH))
 
     c_x1.wait()
     c_li1.wait()
+    f_li1()
     w_x1()
     w_li1()
     for j in range(NPL):
@@ -200,13 +267,7 @@
     w_s2 = spread("row", lambda peer: s2f.at[:, my_rows, :], lambda me: s2f.at[:, aligned(me, SLAB), :])
 
     w_up = spread("col", lambda peer: up.at[:, my_k, :], lambda me: up.at[:, aligned(me, KCH), :])
-    w_ltp1()
-    for b in range(len(L_PAIRS)):
-        ltp[b, my_rows, :] = jnp.concatenate([ltp1[0, b] + ltp1[1, b], ltp1[2, b] + ltp1[3, b]], axis=-1)
-    w_ltp = spread("row", lambda peer: ltp.at[:, my_rows, :], lambda me: ltp.at[:, aligned(me, SLAB), :])
-    for copy in c_uit:
-        copy.wait()
-
+    f_li2()
     w_lp()
     toward = jnp.zeros((TOPL * SLAB, CG), F32)
     for q in range(COLS):
@@ -224,10 +285,26 @@
         block = ylow[NPL:LOC, q * KCH:(q + 1) * KCH, :].reshape(NPL * KCH, CG)
         toward = toward + mm(lp[q, :, NPL * KCH:LOC * KCH], block)
     tt[...] = nt(eye, toward.astype(BF16)).astype(BF16)
-    w_rv = spread("row", lambda peer: tt.at[aligned(peer, CP), :], lambda me: rv.at[me])
-    rv[r] = tt[aligned(r, CP), :]
-
-    w_uit = spread("row", lambda peer: uinvt.at[:, my_rows, :], lambda me: uinvt.at[:, aligned(me, SLAB), :])
+    base = take("r", 2 * ROWS)
+    remote(tt.at[aligned(r, CP), :], rv.at[1, r], base + ROWS, {"gz": partners[0]})
+    for step in range(1, ROWS):
+        peer = lax.rem(r + step, ROWS)
+        remote(tt.at[aligned(peer, CP), :], rv.at[1, r], base + ROWS + step, {"row": peer, "gz": partners[0]})
+        remote(tt.at[aligned(peer, CP), :], rv.at[0, r], base + step, {"row": peer})
+    rv[0, r] = tt[aligned(r, CP), :]
+
+    def w_rv():
+        await_slot(rv.at[1, r], base + ROWS)
+        for step in range(1, ROWS):
+            sender = lax.rem(r + ROWS - step, ROWS)
+            await_slot(rv.at[0, sender], base + step)
+            await_slot(rv.at[1, sender], base + ROWS + step)
+
+    w_ltp1()
+    for b in range(len(L_PAIRS)):
+        ltp[b, my_rows, :] = jnp.concatenate([ltp1[0, b] + ltp1[1, b], ltp1[2, b] + ltp1[3, b]], axis=-1)
+    f_ltp, w_ltp = spread_row_shared(ltp.at[:, my_rows, :], lambda me: ltp.at[:, aligned(me, SLAB), :])
+    f_lit()
 
     slot_of_lane = lax.broadcasted_iota(jnp.int32, (CP, CG), 1) // SLAB
 
@@ -246,49 +323,64 @@
     w_rr()
     rr_tiles = [rr[q].astype(F32) for q in range(ROWS)]
     top_rhs = [by_level(rr_tiles, m) for m in range(TOPL)]
+    w_utp()
+    f_ut, w_ut = spread_row_shared(utp, lambda me: ut.at[:, :, lanes_of(me)])
+    c_ut = local(utp, ut.at[:, :, lanes_of(r)])
     w_rv()
-    rv_tiles = [rv[q].astype(F32) for q in range(ROWS)]
+    rv_tiles = [rv[0, q].astype(F32) + rv[1, q].astype(F32) for q in range(ROWS)]
     pend = [by_level(rv_tiles, m) for m in range(TOPL)]
+    f_ltp()
+    w_lit()
+    w_ltp()
 
     top_y = []
-    w_us = w_ut = None
     for a in range(TOPL):
         count = TOPL - a
         base = Z_BASE[a]
-        for m in range(a, TOPL):
-            zs[base + m - a] = pend[m].astype(BF16)
-        slot = take("r")
-        remote(zs.at[pl.ds(base, count)], zr.at[pl.ds(base, count)], slot, {"gz": partners[a]})
-        if a == 0:
-            c_ui2.wait()
-            w_ui2 = spread("row", lambda peer: uinv2.at[:, my_rows, :], lambda me: uinv2.at[:, aligned(me, SLAB), :])
-            w_up()
-            u_lanes = pl.ds(pl.multiple_of(r * CG, CG), CG)
-            w_ut = spread(
-                "row", lambda peer: up.at[pl.ds(LOC + 1, 2)],
-                lambda me: ut.at[:, :, pl.ds(pl.multiple_of(me * CG, CG), CG)],
-            )
-            w_us = spread(
-                "row", lambda peer: up.at[pl.ds(0, LOC + 1), aligned(peer, SLAB), :],
-                lambda me: us.at[:, :, pl.ds(pl.multiple_of(me * CG, CG), CG)],
-            )
-            c_ut = local(up.at[pl.ds(LOC + 1, 2)], ut.at[:, :, u_lanes])
-            c_us = local(up.at[pl.ds(0, LOC + 1), my_rows, :], us.at[:, :, u_lanes])
-            w_lit()
-            w_ltp()
-        await_slot(zr.at[pl.ds(base, count)], slot)
-        for m in range(a, TOPL):
-            pend[m] = pend[m] + zr[base + m - a].astype(F32)
+        if a > 0:
+            place = pl.ds(base, count)
+            for m in range(a, TOPL):
+                zs[base + m - a] = pend[m].astype(BF16)
+            slot = take("r")
+            if a < TOPL - 1:
+                remote(zs.at[place], zr.at[place], slot, {"gz": partners[a]})
+            else:
+                last_sends = [
+                    pltpu.make_async_remote_copy(
+                        src_ref=zs.at[place], dst_ref=zr.at[place], send_sem=ssem.at[take("s")],
+                        recv_sem=rsem.at[slot], device_id={"gz": first_target + step}, device_id_type=MESH,
+                    )
+                    for step in range(4)
+                ]
+
+                @pl.when(edge)
+                def _():
+                    for copy in last_sends:
+                        copy.start()
+
+            if a == 1:
+                f_uit()
+                f_ui2()
+                w_up()
+                w_us = spread(
+                    "row", lambda peer: up.at[:, aligned(peer, SLAB), :], lambda me: us.at[:, :, lanes_of(me)]
+                )
+                c_us = local(up.at[:, my_rows, :], us.at[:, :, lanes_of(r)])
+            if a == 3:
+                f_ut()
+            await_slot(zr.at[place], slot)
+            for m in range(a, TOPL):
+                pend[m] = pend[m] + zr[base + m - a].astype(F32)
         solved = nt((top_rhs[a] - pend[a]).astype(BF16), linvt[a])
         top_y.append(solved)
         low = solved.astype(BF16)
-        for b, (source, m) in enumerate(L_PAIRS):
-            if source == a:
+        for b, (below, m) in enumerate(L_PAIRS):
+            if below == a:
                 pend[m] = pend[m] + nt(low, ltp[b])
 
+    w_uit()
     c_ut.wait()
     w_ut()
-    w_uit()
     tiles = [jnp.zeros((CP, CG), F32) for _ in range(ROWS)]
     for a in reversed(range(TOPL)):
         value = top_y[a]
@@ -309,6 +401,9 @@
     xp[my_cp, :] = jnp.concatenate(tiles, axis=-1).astype(BF16)
     w_xp = spread("row", lambda peer: xp.at[my_cp, :], lambda me: xp.at[aligned(me, CP), :])
 
+    lane_slot = lax.rem(lax.broadcasted_iota(jnp.int32, (W, ROWS * CG), 1) // SLAB, NPL)
+    for j in range(NPL):
+        tree_w[j] = jnp.where(lane_slot == j, ut[2], jnp.zeros((W, ROWS * CG), BF16))
     c_us.wait()
     w_us()
     w_xp()
@@ -319,7 +414,11 @@
         sb2[i, my_rows, :] = value.astype(BF16)
     w_sb2 = spread("row", lambda peer: sb2.at[:, my_rows, :], lambda me: sb2.at[:, aligned(me, SLAB), :])
     path_term1 = nt(us[0:NPL].reshape(NPL * SLAB, ROWS * CG), path)
-    own_path = nt(eye, xp[:, pl.ds(pl.multiple_of(r * CG, CG), CG)])
+    for j in range(NPL):
+        value = y[j, my_rows, :] - path_term1[j * SLAB:(j + 1) * SLAB, :]
+        sb1[j, my_rows, :] = value.astype(BF16)
+    w_sb1 = spread("row", lambda peer: sb1.at[:, my_rows, :], lambda me: sb1.at[:, aligned(me, SLAB), :])
+    own_path = nt(eye, xp[:, lanes_of(r)])
     for m in range(TOPL):
         out_p[m] = own_path[m * SLAB:(m + 1) * SLAB, :]
     piece_rows = SLAB // COLS
@@ -328,14 +427,9 @@
         return pl.ds(pl.multiple_of(peer * piece_rows, piece_rows), piece_rows)
 
     w_outp = spread(
-        "col", lambda peer: out_p.at[:, out_rows(peer), :],
-        lambda me: x_path.at[0, :, :, pl.ds(pl.multiple_of(me * CG, CG), CG)],
+        "col", lambda peer: out_p.at[:, out_rows(peer), :], lambda me: x_path.at[0, :, :, lanes_of(me)]
     )
     c_outp = local(out_p.at[:, out_rows(c), :], x_path.at[0, :, :, my_cols])
-    lane_slot = lax.rem(lax.broadcasted_iota(jnp.int32, (SLAB, ROWS * CG), 1) // SLAB, NPL)
-    tree_piece = us[LOC]
-    tree_blocks = [jnp.where(lane_slot == j, tree_piece, jnp.zeros_like(tree_piece)) for j in range(NPL)]
-    tree_weights = jnp.concatenate(tree_blocks, axis=0)
 
     w_ui2()
     c_uiown.wait()
@@ -344,27 +438,21 @@
         x2low[i] = mm(uinv2[i], sb2[i]).astype(BF16)
     parent_x = [x2low[parent[j]].reshape(ROWS, 1, SLAB, CG) for j in range(NPL)]
     stacked = jnp.concatenate(parent_x, axis=1).reshape(ROWS * NPL * SLAB, CG)
-    tree_term = mm(tree_weights, stacked)
-    for j in range(NPL):
-        rows = slice(j * SLAB, (j + 1) * SLAB)
-        value = y[j, my_rows, :] - path_term1[rows, :] - tree_term[rows, :]
-        sb1[j, my_rows, :] = value.astype(BF16)
-    w_sb1 = spread("row", lambda peer: sb1.at[:, my_rows, :], lambda me: sb1.at[:, aligned(me, SLAB), :])
+    trees = [mm(tree_w[j], stacked) for j in range(NPL)]
     for i in range(NPL):
         out_l[NPL + i] = mm(uinv_own[NPL + i], sb2[i])
 
     def send_out(first):
         part = pl.ds(first, NPL)
         wait = spread(
-            "col", lambda peer: out_l.at[part, out_rows(peer), :],
-            lambda me: x_local.at[part, :, pl.ds(pl.multiple_of(me * CG, CG), CG)],
+            "col", lambda peer: out_l.at[part, out_rows(peer), :], lambda me: x_local.at[part, :, lanes_of(me)]
         )
         return wait, local(out_l.at[part, out_rows(c), :], x_local.at[part, :, my_cols])
 
     w_out2, c_out2 = send_out(NPL)
     w_sb1()
     for j in range(NPL):
-        out_l[j] = mm(uinv_own[j], sb1[j])
+        out_l[j] = mm(uinv_own[j], (sb1[j].astype(F32) - trees[j]).astype(BF16))
     w_out1, c_out1 = send_out(0)
     w_outp()
     w_out2()
@@ -373,6 +461,11 @@
         copy.wait()
     for copy in pending_sends:
         copy.wait_send()
+
+    @pl.when(edge)
+    def _():
+        for copy in last_sends:
+            copy.wait_send()
 
 
 def per_device(*arrays):
@@ -400,14 +493,16 @@
         vmem((TOPL, W, W), BF16),
         vmem((TOPL, W, W), BF16),
         vmem((NPL, W, W), BF16),
-        vmem((LOC + 3, W, CG), BF16),
-        vmem((LOC + 1, SLAB, ROWS * CG), BF16),
-        vmem((2, W, ROWS * CG), BF16),
+        vmem((LOC, W, CG), BF16),
+        vmem((LOC, SLAB, ROWS * CG), BF16),
+        vmem((3, W, CG), BF16),
+        vmem((3, W, ROWS * CG), BF16),
+        vmem((NPL, W, ROWS * CG), BF16),
         vmem((LOC, W, CG), F32),
         vmem((LOC, W, CG), BF16),
         vmem((NPL, W, CG), BF16),
         vmem((CG, TOPL * SLAB), BF16),
-        vmem((ROWS, CP, CG), BF16),
+        vmem((2, ROWS, CP, CG), BF16),
         vmem((CG, TOPL * SLAB), BF16),
         vmem((ROWS, CP, CG), BF16),
         vmem((10, CP, W), BF16),
@@ -419,8 +514,8 @@
         vmem((LOC, SLAB, CG), F32),
         vmem((TOPL, SLAB, CG), F32),
         pltpu.SemaphoreType.DMA((48,)),
-        pltpu.SemaphoreType.DMA((160,)),
-        pltpu.SemaphoreType.DMA((160,)),
+        pltpu.SemaphoreType.DMA((200,)),
+        pltpu.SemaphoreType.DMA((200,)),
     ]
     return pl.pallas_call(
         kernel,

time: 104 us -> 78.3 us (0.75)
  Pallas kernels: 101 us -> 75.2 us
    pallas_call x1, Pallas kernels: 101 us -> 75.2 us  [per_device(): pl.pallas_call(kernel, out_shape=(jax.ShapeDtypeStruct((LOC, SLAB // COLS...]
where the time goes in v2:
time: 78.3 us; the launch traced here: 78.1 us
  Pallas kernels  75.2 us (96%)
  local copies, waits for them, and re-layouts  2.23 us (3%)
    pallas_call x1, Pallas kernels, per_device(): pl.pallas_call(kernel, out_shape=(jax.ShapeDtypeStruct((LOC, SLAB // COLS...  75.2 us
    unnamed x4, local copies, waits for them, and re-layouts  2.23 us

profile of v2, /device:TPU:1, one launch (start us, length us, event | category | flops | bytes accessed | tf_op | source)
XLA Modules:
  0.0 78.1 jit_solution(3939061051018866812)
XLA Ops:
  0.6 75.2 %shard_map.140 = (f32[8,8,512]{2,1,0:T(8,128)}, f32[1,4,8,512]{3,2,1,0:T(8,128)}) custom-call(s32[4]{0:T(128)} %parent.1, bf16[4,32,64]{2,1,0:T(8,128)(2,1)} %l_tree.1, bf16[8,4,32,64]{3,2,1,0:T(8,128)(2,1)} %l_path.1, bf16[15,4,32,64]{3,2,1,0:T(8,128)(2,1)} %l_top.1, bf16[4,32,64]{2,1,0:T(8,128)(2,1)} %bitcast.5, bf16[8,4,32,64]{3,2,1,0:T(8,128)(2,1)} %bitcast.4, ...), custom_call_target="tpu_custom_call" | custom-call | tf_op jit(solution)/shard_map/pallas_call | solution.py:520
  75.9 0.0 copy-start
  75.9 1.6 %copy.17 = f32[8,8,512]{2,1,0:T(8,128)} copy(f32[8,8,512]{2,1,0:T(8,128)} %get-tuple-element.4) | data formatting | bytes 262144
  77.5 0.0 copy-done
  77.5 0.6 copy.18
Async XLA Ops:
  75.9 1.6 %copy-start = (f32[1,4,8,512]{3,2,1,0:T(8,128)S(1)}, f32[1,4,8,512]{3,2,1,0:T(8,128)}, u32[]{:S(2)}) copy-start(f32[1,4,8,512]{3,2,1,0:T(8,128)} %get-tuple-element.5) | copy-start | bytes 196612

commit v3 on v2

--- a/solution.py
+++ b/solution.py
@@ -16,8 +16,8 @@
 SLAB, KCH = W // ROWS, W // COLS
 CG = R // COLS
 CP = CG // ROWS
-L_PAIRS = ((0, 1), (0, 2), (0, 3), (1, 2), (1, 3), (2, 3))
-Z_BASE = (0, 4, 7, 9)
+L_PAIRS = ((0, 1), (0, 2), (0, 3), (1, 2), (1, 3), (2, 3), (3, 3), (3, 3))
+QUAD = 4
 
 
 def nt(a, b):
@@ -36,8 +36,8 @@
     parent, l_tree, l_path, l_top, u_tree, u_path, u_top, linv_local, linv_top, uinv_local,
     uinv_top, rhs_local, rhs_top, x_local, x_path,
     st_ltree, st_lpath, st_ltop, st_utree, st_upath, st_utop, uinv_own, rhs2_own, st_rt,
-    x1, linv, lt, lp, ltp1, ltp, linvt, uinvt, uinv2, up, us, utp, ut, tree_w,
-    y, ylow, s2f, tt, rv, rt, rr, zs, zr, xp, sb2, x2low, sb1, out_l, out_p,
+    x1, linv, lt, lp, ltp1, ltp, linvt, uinvt, uinv2, up, us, utp, ut, tree_w, mprod, vprod, nprod,
+    y, ylow, s2f, tt, rv, rt, rr, zs1, zr1, zs2, zr2, xp, sb2, x2low, sb1, out_l, out_p,
     lsem, ssem, rsem,
 ):
     r = lax.axis_index("row")
@@ -125,6 +125,7 @@
         return forward, wait
 
     anc = [LAYERS - (LAYERS >> a) + g // 2 ** (a + 1) for a in range(TOPL)]
+    other = LAYERS - (LAYERS >> 2) + 1 - g // (LAYERS // 2)
     my_rows = aligned(r, SLAB)
     my_k = aligned(c, KCH)
     my_cols = aligned(c, CG)
@@ -136,37 +137,54 @@
     def lanes_of(owner):
         return pl.ds(pl.multiple_of(owner * CG, CG), CG)
 
+    c_ltree = local(l_tree, st_ltree)
+    c_lpath = local(l_path, st_lpath)
+    c_ltop = [local(l_top.at[node], st_ltop.at[n]) for n, node in enumerate(anc[0:3] + [other])]
+
     barrier = pltpu.get_barrier_semaphore()
 
     def greet(target):
         pl.semaphore_signal(barrier, inc=1, device_id=target, device_id_type=MESH)
 
-    partners = []
-    for a in range(TOPL - 1):
-        span = 2**a
-        partners.append(g + span - 2 * span * lax.rem(g // span, 2))
-    quarter = g // 4
-    source = jnp.where(quarter == 0, 15, jnp.where(quarter == 1, 8, jnp.where(quarter == 2, 7, 0)))
-    edge = jnp.logical_or(jnp.logical_or(g == 0, g == 7), jnp.logical_or(g == 8, g == 15))
-    first_target = jnp.where(g == 0, 12, jnp.where(g == 7, 8, jnp.where(g == 8, 4, 0)))
+    near = g + 1 - 2 * lax.rem(g, 2)
+    across = g + 2 - 4 * lax.rem(g // 2, 2)
+    quad, place_in_quad = g // QUAD, lax.rem(g, QUAD)
+    quads = LAYERS // QUAD
+    upper = place_in_quad // (QUAD - 1)
+    speaks = jnp.logical_or(place_in_quad == 0, place_in_quad == QUAD - 1)
+    half = place_in_quad // 2
+
+    def quad_at(offset):
+        return lax.rem(quad + quads + offset, quads) * QUAD
+
+    sources = [quad_at(1), quad_at(-1) + QUAD - 1, quad_at(2) + (QUAD - 1) * (1 - half)]
+    direction = 2 * upper - 1
+    targets = [(quad_at(2) + 2 * (1 - upper) + step, 2) for step in range(2)]
+    targets += [(quad_at(direction) + step, upper) for step in range(QUAD)]
+    for source in sources:
+        greet({"gz": source})
+    greet({"gz": across})
+    for step in range(ROWS):
+        greet({"row": lax.rem(r + step, ROWS), "gz": near})
     for step in range(1, ROWS):
         greet({"row": lax.rem(r + step, ROWS)})
-    for step in range(ROWS):
-        greet({"row": lax.rem(r + step, ROWS), "gz": partners[0]})
     for step in range(1, COLS):
         greet({"col": lax.rem(c + step, COLS)})
-    greet({"gz": partners[1]})
-    greet({"gz": partners[2]})
-    greet({"gz": source})
-
+
+    pl.semaphore_wait(barrier, ROWS - 1 + ROWS + COLS - 1 + 1 + jnp.where(speaks, 6, 0))
+
+    w_x1 = spread(
+        "row", lambda peer: rhs_local.at[pl.ds(0, NPL), :, my_cols],
+        lambda me: x1.at[:, aligned(me, SLAB), :],
+    )
+    f_li1, w_li1 = spread_col_shared(
+        linv_local.at[pl.ds(0, NPL), half_src], lambda o, h: linv.at[pl.ds(0, NPL), half_rows(o, h), :]
+    )
     c_x1 = local(rhs_local.at[pl.ds(0, NPL), :, my_cols], x1.at[:, my_rows, :])
     c_li1 = local(linv_local.at[pl.ds(0, NPL)], linv.at[pl.ds(0, NPL), my_k, :])
-    c_ltree = local(l_tree, st_ltree)
-    c_lpath = local(l_path, st_lpath)
-    c_ltop = [local(l_top.at[anc[a]], st_ltop.at[a]) for a in range(3)]
-    c_lit = [local(linv_top.at[anc[a]], linvt.at[a, my_k, :]) for a in range(TOPL)]
+    c_lit = [local(linv_top.at[node], linvt.at[n, my_k, :]) for n, node in enumerate(anc + [other])]
     c_uit = [local(uinv_top.at[anc[a]], uinvt.at[a, my_rows, :]) for a in range(TOPL)]
-    c_rt = [local(rhs_top.at[anc[a], :, my_cols], st_rt.at[a]) for a in range(TOPL)]
+    c_rt = [local(rhs_top.at[node, :, my_cols], st_rt.at[n]) for n, node in enumerate(anc + [other])]
     c_li2 = local(linv_local.at[pl.ds(NPL, NPL)], linv.at[pl.ds(NPL, NPL), my_k, :])
     c_rhs2 = local(rhs_local.at[pl.ds(NPL, NPL), :, my_cols], rhs2_own)
     c_utop = [local(u_top.at[anc[a]], st_utop.at[a]) for a in range(3)]
@@ -175,27 +193,16 @@
     c_ui2 = local(uinv_local.at[pl.ds(NPL, NPL)], uinv2.at[:, my_rows, :])
     c_uiown = local(uinv_local, uinv_own)
 
-    pl.semaphore_wait(barrier, ROWS - 1 + ROWS + COLS - 1 + 2 + jnp.where(edge, 4, 0))
-
-    w_x1 = spread(
-        "row", lambda peer: rhs_local.at[pl.ds(0, NPL), :, my_cols],
-        lambda me: x1.at[:, aligned(me, SLAB), :],
-    )
-    f_li1, w_li1 = spread_col_shared(
-        linv_local.at[pl.ds(0, NPL), half_src], lambda o, h: linv.at[pl.ds(0, NPL), half_rows(o, h), :]
-    )
-    odd = lax.rem(c, 2)
-
-    def shifted(block):
-        blank = jnp.zeros_like(block)
-        low = jnp.concatenate([block, blank], axis=-1)
-        high = jnp.concatenate([blank, block], axis=-1)
-        return jnp.where(odd == 0, low, high)
-
     c_ltree.wait()
-    for j in range(NPL):
-        lt[c, j] = shifted(st_ltree[j])
+    for b in range(NPL // 2):
+        lt[c, b] = jnp.concatenate([st_ltree[2 * b], st_ltree[2 * b + 1]], axis=-1)
     w_lt = spread("col", lambda peer: lt.at[c], lambda me: lt.at[me])
+    for copy in c_ltop:
+        copy.wait()
+    for b in range(len(L_PAIRS) // 2):
+        (a1, m1), (a2, m2) = L_PAIRS[2 * b], L_PAIRS[2 * b + 1]
+        ltp1[c, b] = jnp.concatenate([st_ltop[a1, m1], st_ltop[a2, m2]], axis=-1)
+    w_ltp1 = spread("col", lambda peer: ltp1.at[c], lambda me: ltp1.at[me])
     f_li2, w_li2 = spread_col_shared(
         linv_local.at[pl.ds(NPL, NPL), half_src], lambda o, h: linv.at[pl.ds(NPL, NPL), half_rows(o, h), :]
     )
@@ -203,11 +210,11 @@
     for m in range(TOPL):
         lp[c, pl.ds(m * SLAB, SLAB), :] = jnp.concatenate([st_lpath[k, m] for k in range(LOC)], axis=-1)
     w_lp = spread("col", lambda peer: lp.at[c], lambda me: lp.at[me])
-    for copy in c_ltop:
-        copy.wait()
-    for b, (a, m) in enumerate(L_PAIRS):
-        ltp1[c, b] = shifted(st_ltop[a, m])
-    w_ltp1 = spread("col", lambda peer: ltp1.at[c], lambda me: ltp1.at[me])
+
+    def unpaired(pieces, b):
+        half = pl.ds(b % 2 * KCH, KCH)
+        return jnp.concatenate([pieces[q, b // 2, :, half] for q in range(COLS)], axis=-1)
+
     for copy in c_lit:
         copy.wait()
     f_lit, w_lit = spread_col_shared(
@@ -217,32 +224,8 @@
         copy.wait()
     f_uit, w_uit = spread_row_shared(uinvt.at[:, my_rows, :], lambda me: uinvt.at[:, aligned(me, SLAB), :])
 
-    eye = (
-        lax.broadcasted_iota(jnp.int32, (CG, CG), 0) == lax.broadcasted_iota(jnp.int32, (CG, CG), 1)
-    ).astype(F32).astype(BF16)
-    for copy in c_rt:
-        copy.wait()
-    rt[...] = nt(eye, st_rt[...].reshape(TOPL * SLAB, CG)).astype(BF16)
-    w_rr = spread("row", lambda peer: rt.at[aligned(peer, CP), :], lambda me: rr.at[me])
-    rr[r] = rt[aligned(r, CP), :]
     c_ui2.wait()
     f_ui2, w_ui2 = spread_row_shared(uinv2.at[:, my_rows, :], lambda me: uinv2.at[:, aligned(me, SLAB), :])
-
-    eye_k = eye[0:KCH, 0:KCH]
-
-    def packed(stack):
-        return nt(eye_k, stack).astype(BF16)
-
-    for copy in c_utop:
-        copy.wait()
-    utp[0, my_k, :] = packed(jnp.concatenate([st_utop[2, 3], st_utop[0, 1], st_utop[0, 2], st_utop[0, 3]], axis=0))
-    utp[1, my_k, :] = packed(st_utop[1].reshape(CG, KCH))
-    c_utree.wait()
-    utp[2, my_k, :] = packed(st_utree[...].reshape(CG, KCH))
-    w_utp = spread("col", lambda peer: utp.at[:, my_k, :], lambda me: utp.at[:, aligned(me, KCH), :])
-    c_upath.wait()
-    for k in range(LOC):
-        up[k, my_k, :] = packed(st_upath[k].reshape(CG, KCH))
 
     c_x1.wait()
     c_li1.wait()
@@ -256,8 +239,7 @@
     w_lt()
     terms = []
     for j in range(NPL):
-        term = mm(lt[0, j] + lt[1, j], ylow[j, 0:CG, :]) + mm(lt[2, j] + lt[3, j], ylow[j, CG:W, :])
-        terms.append(term)
+        terms.append(mm(unpaired(lt, j), ylow[j]))
     c_rhs2.wait()
     for i in range(NPL):
         value = rhs2_own[i].astype(F32)
@@ -266,8 +248,38 @@
         s2f[i, my_rows, :] = value.astype(BF16)
     w_s2 = spread("row", lambda peer: s2f.at[:, my_rows, :], lambda me: s2f.at[:, aligned(me, SLAB), :])
 
+    eye = (
+        lax.broadcasted_iota(jnp.int32, (CG, CG), 0) == lax.broadcasted_iota(jnp.int32, (CG, CG), 1)
+    ).astype(F32).astype(BF16)
+    for copy in c_rt:
+        copy.wait()
+    rt[:, 0:CG] = nt(eye, st_rt[0:TOPL].reshape(TOPL * SLAB, CG)).astype(BF16)
+    rt[:, CG:2 * CG] = nt(eye, jnp.concatenate([st_rt[TOPL]] * 4, axis=0)).astype(BF16)
+    w_rr = spread("row", lambda peer: rt.at[aligned(peer, CP), :], lambda me: rr.at[me])
+    rr[r] = rt[aligned(r, CP), :]
+    w_ltp1()
+    for b in range(len(L_PAIRS) - 1):
+        ltp[b, my_rows, :] = unpaired(ltp1, b)
+    f_ltp, w_ltp = spread_row_shared(ltp.at[:, my_rows, :], lambda me: ltp.at[:, aligned(me, SLAB), :])
+    f_li2()
+
+    eye_k = eye[0:KCH, 0:KCH]
+
+    def packed(stack):
+        return nt(eye_k, stack).astype(BF16)
+
+    for copy in c_utop:
+        copy.wait()
+    utp[0, my_k, :] = packed(jnp.concatenate([st_utop[2, 3], st_utop[0, 1], st_utop[0, 2], st_utop[0, 3]], axis=0))
+    utp[1, my_k, :] = packed(st_utop[1].reshape(CG, KCH))
+    c_utree.wait()
+    utp[2, my_k, :] = packed(st_utree[...].reshape(CG, KCH))
+    w_utp = spread("col", lambda peer: utp.at[:, my_k, :], lambda me: utp.at[:, aligned(me, KCH), :])
+    c_upath.wait()
+    for k in range(LOC):
+        up[k, my_k, :] = packed(st_upath[k].reshape(CG, KCH))
+
     w_up = spread("col", lambda peer: up.at[:, my_k, :], lambda me: up.at[:, aligned(me, KCH), :])
-    f_li2()
     w_lp()
     toward = jnp.zeros((TOPL * SLAB, CG), F32)
     for q in range(COLS):
@@ -286,10 +298,10 @@
         toward = toward + mm(lp[q, :, NPL * KCH:LOC * KCH], block)
     tt[...] = nt(eye, toward.astype(BF16)).astype(BF16)
     base = take("r", 2 * ROWS)
-    remote(tt.at[aligned(r, CP), :], rv.at[1, r], base + ROWS, {"gz": partners[0]})
+    remote(tt.at[aligned(r, CP), :], rv.at[1, r], base + ROWS, {"gz": near})
     for step in range(1, ROWS):
         peer = lax.rem(r + step, ROWS)
-        remote(tt.at[aligned(peer, CP), :], rv.at[1, r], base + ROWS + step, {"row": peer, "gz": partners[0]})
+        remote(tt.at[aligned(peer, CP), :], rv.at[1, r], base + ROWS + step, {"row": peer, "gz": near})
         remote(tt.at[aligned(peer, CP), :], rv.at[0, r], base + step, {"row": peer})
     rv[0, r] = tt[aligned(r, CP), :]
 
@@ -300,13 +312,9 @@
             await_slot(rv.at[0, sender], base + step)
             await_slot(rv.at[1, sender], base + ROWS + step)
 
-    w_ltp1()
-    for b in range(len(L_PAIRS)):
-        ltp[b, my_rows, :] = jnp.concatenate([ltp1[0, b] + ltp1[1, b], ltp1[2, b] + ltp1[3, b]], axis=-1)
-    f_ltp, w_ltp = spread_row_shared(ltp.at[:, my_rows, :], lambda me: ltp.at[:, aligned(me, SLAB), :])
     f_lit()
 
-    slot_of_lane = lax.broadcasted_iota(jnp.int32, (CP, CG), 1) // SLAB
+    slot_of_lane = lax.shift_right_logical(lax.broadcasted_iota(jnp.int32, (CP, CG), 1), 5)
 
     def by_level(tiles, m):
         halves = []
@@ -321,77 +329,91 @@
         return jnp.concatenate(halves, axis=-1)
 
     w_rr()
-    rr_tiles = [rr[q].astype(F32) for q in range(ROWS)]
+    rr_tiles = [rr[q, :, 0:CG].astype(F32) for q in range(ROWS)]
     top_rhs = [by_level(rr_tiles, m) for m in range(TOPL)]
+    top_rhs.append(by_level([rr[q, :, CG:2 * CG].astype(F32) for q in range(ROWS)], 0))
+    f_ltp()
+    w_rv()
+    rv_tiles = [rv[0, q].astype(F32) + rv[1, q].astype(F32) for q in range(ROWS)]
+    pend = [by_level(rv_tiles, m) for m in range(TOPL)]
+    w_lit()
+    w_ltp()
+
+    def solve_zero():
+        solved = nt((top_rhs[0] - pend[0]).astype(BF16), linvt[0])
+        low = solved.astype(BF16)
+        for m in range(1, TOPL):
+            pend[m] = pend[m] + nt(low, ltp[m - 1])
+        return low
+
+    y_low = [solve_zero()]
+    for m in range(1, TOPL):
+        zs1[m - 1] = pend[m].astype(BF16)
+    slot = take("r")
+    remote(zs1, zr1, slot, {"gz": across})
     w_utp()
     f_ut, w_ut = spread_row_shared(utp, lambda me: ut.at[:, :, lanes_of(me)])
     c_ut = local(utp, ut.at[:, :, lanes_of(r)])
-    w_rv()
-    rv_tiles = [rv[0, q].astype(F32) + rv[1, q].astype(F32) for q in range(ROWS)]
-    pend = [by_level(rv_tiles, m) for m in range(TOPL)]
-    f_ltp()
-    w_lit()
-    w_ltp()
-
-    top_y = []
-    for a in range(TOPL):
-        count = TOPL - a
-        base = Z_BASE[a]
-        if a > 0:
-            place = pl.ds(base, count)
-            for m in range(a, TOPL):
-                zs[base + m - a] = pend[m].astype(BF16)
-            slot = take("r")
-            if a < TOPL - 1:
-                remote(zs.at[place], zr.at[place], slot, {"gz": partners[a]})
-            else:
-                last_sends = [
-                    pltpu.make_async_remote_copy(
-                        src_ref=zs.at[place], dst_ref=zr.at[place], send_sem=ssem.at[take("s")],
-                        recv_sem=rsem.at[slot], device_id={"gz": first_target + step}, device_id_type=MESH,
-                    )
-                    for step in range(4)
-                ]
-
-                @pl.when(edge)
-                def _():
-                    for copy in last_sends:
-                        copy.start()
-
-            if a == 1:
-                f_uit()
-                f_ui2()
-                w_up()
-                w_us = spread(
-                    "row", lambda peer: up.at[:, aligned(peer, SLAB), :], lambda me: us.at[:, :, lanes_of(me)]
-                )
-                c_us = local(up.at[:, my_rows, :], us.at[:, :, lanes_of(r)])
-            if a == 3:
-                f_ut()
-            await_slot(zr.at[place], slot)
-            for m in range(a, TOPL):
-                pend[m] = pend[m] + zr[base + m - a].astype(F32)
-        solved = nt((top_rhs[a] - pend[a]).astype(BF16), linvt[a])
-        top_y.append(solved)
-        low = solved.astype(BF16)
-        for b, (below, m) in enumerate(L_PAIRS):
-            if below == a:
-                pend[m] = pend[m] + nt(low, ltp[b])
-
+    f_uit()
+    f_ui2()
+    for n, (b, node) in enumerate(((3, 1), (4, 1), (5, 2), (6, 4))):
+        mprod[n] = mm(ltp[b], linvt[node]).astype(BF16)
+    await_slot(zr1, slot)
+    for m in range(1, TOPL):
+        pend[m] = pend[m] + zr1[m - 1].astype(F32)
+
+    low = (top_rhs[1] - pend[1]).astype(BF16)
+    for m in range(2, TOPL):
+        pend[m] = pend[m] + nt(low, mprod[m - 2])
+        zs2[m - 2] = pend[m].astype(BF16)
+    slot = take("r", 3)
+    speeches = [
+        pltpu.make_async_remote_copy(
+            src_ref=zs2, dst_ref=zr2.at[where], send_sem=ssem.at[take("s")],
+            recv_sem=rsem.at[slot + where], device_id={"gz": target}, device_id_type=MESH,
+        )
+        for target, where in targets
+    ]
+
+    @pl.when(speaks)
+    def _():
+        for copy in speeches:
+            copy.start()
+
+    y_low.append(nt(low, linvt[1]).astype(BF16))
+    w_up()
+    w_us = spread("row", lambda peer: up.at[:, aligned(peer, SLAB), :], lambda me: us.at[:, :, lanes_of(me)])
+    c_us = local(up.at[:, my_rows, :], us.at[:, :, lanes_of(r)])
     w_uit()
+    vprod[...] = mm(uinvt[TOPL - 1], linvt[TOPL - 1]).astype(BF16)
+    known_x = [nt(y_low[n], uinvt[n]) for n in range(2)]
+    f_ut()
     c_ut.wait()
     w_ut()
+    for n, tile in enumerate((0, 1, 0)):
+        nprod[n] = mm(uinvt[n], ut[tile]).astype(BF16)
+    for where in range(3):
+        await_slot(zr2.at[where], slot + where)
+    even = lax.rem(quad, 2) == 0
+    after, before, opposite = (zr2[where, 0].astype(F32) for where in range(3))
+    own_sum = pend[2] + jnp.where(even, after, before)
+    other_sum = opposite + jnp.where(even, before, after)
+    root_sum = pend[3] + zr2[0, 1].astype(F32) + zr2[1, 1].astype(F32) + zr2[2, 1].astype(F32)
+    low = (top_rhs[2] - own_sum).astype(BF16)
+    root_sum = root_sum + nt(low, mprod[2]) + nt((top_rhs[4] - other_sum).astype(BF16), mprod[3])
+    known_x.append(nt(nt(low, linvt[2]).astype(BF16), uinvt[2]))
+    known_x.append(nt((top_rhs[3] - root_sum).astype(BF16), vprod[...]))
+
     tiles = [jnp.zeros((CP, CG), F32) for _ in range(ROWS)]
     for a in reversed(range(TOPL)):
-        value = top_y[a]
+        solved = known_x[a]
         if a < TOPL - 1:
             if a == 2:
                 known = [pltpu.roll(tile, SLAB, 1) for tile in tiles]
             else:
                 known = tiles
             above = jnp.concatenate(known, axis=-1).astype(BF16)
-            value = value - nt(above, ut[0 if a != 1 else 1])
-        solved = nt(value.astype(BF16), uinvt[a])
+            solved = solved - nt(above, nprod[a])
         for q in range(2):
             half = solved[:, q * CG:(q + 1) * CG]
             for s in range(4):
@@ -401,9 +423,11 @@
     xp[my_cp, :] = jnp.concatenate(tiles, axis=-1).astype(BF16)
     w_xp = spread("row", lambda peer: xp.at[my_cp, :], lambda me: xp.at[aligned(me, CP), :])
 
-    lane_slot = lax.rem(lax.broadcasted_iota(jnp.int32, (W, ROWS * CG), 1) // SLAB, NPL)
+    lane_slot = lax.shift_right_logical(lax.broadcasted_iota(jnp.int32, (8, CG), 1), 5)
     for j in range(NPL):
-        tree_w[j] = jnp.where(lane_slot == j, ut[2], jnp.zeros((W, ROWS * CG), BF16))
+        mask = jnp.where(lane_slot == j, 1.0, 0.0).astype(F32)[0:1, :].astype(BF16)
+        for q in range(ROWS):
+            tree_w[j, :, q * CG:(q + 1) * CG] = ut[2, :, q * CG:(q + 1) * CG] * mask
     c_us.wait()
     w_us()
     w_xp()
@@ -412,12 +436,12 @@
     for i in range(NPL):
         value = y[NPL + i, my_rows, :] - path_term2[i * SLAB:(i + 1) * SLAB, :]
         sb2[i, my_rows, :] = value.astype(BF16)
-    w_sb2 = spread("row", lambda peer: sb2.at[:, my_rows, :], lambda me: sb2.at[:, aligned(me, SLAB), :])
+    f_sb2, w_sb2 = spread_row_shared(sb2.at[:, my_rows, :], lambda me: sb2.at[:, aligned(me, SLAB), :])
     path_term1 = nt(us[0:NPL].reshape(NPL * SLAB, ROWS * CG), path)
     for j in range(NPL):
         value = y[j, my_rows, :] - path_term1[j * SLAB:(j + 1) * SLAB, :]
         sb1[j, my_rows, :] = value.astype(BF16)
-    w_sb1 = spread("row", lambda peer: sb1.at[:, my_rows, :], lambda me: sb1.at[:, aligned(me, SLAB), :])
+    f_sb1, w_sb1 = spread_row_shared(sb1.at[:, my_rows, :], lambda me: sb1.at[:, aligned(me, SLAB), :])
     own_path = nt(eye, xp[:, lanes_of(r)])
     for m in range(TOPL):
         out_p[m] = own_path[m * SLAB:(m + 1) * SLAB, :]
@@ -433,6 +457,8 @@
 
     w_ui2()
     c_uiown.wait()
+    f_sb2()
+    f_sb1()
     w_sb2()
     for i in range(NPL):
         x2low[i] = mm(uinv2[i], sb2[i]).astype(BF16)
@@ -462,9 +488,9 @@
     for copy in pending_sends:
         copy.wait_send()
 
-    @pl.when(edge)
+    @pl.when(speaks)
     def _():
-        for copy in last_sends:
+        for copy in speeches:
             copy.wait_send()
 
 
@@ -477,20 +503,20 @@
     scratch = [
         vmem((NPL, SLAB, KCH), BF16),
         vmem((LOC, TOPL, SLAB, KCH), BF16),
-        vmem((3, TOPL, SLAB, KCH), BF16),
+        vmem((4, TOPL, SLAB, KCH), BF16),
         vmem((NPL, SLAB, KCH), BF16),
         vmem((LOC, TOPL, SLAB, KCH), BF16),
         vmem((3, TOPL, SLAB, KCH), BF16),
         vmem((LOC, SLAB, W), BF16),
         vmem((NPL, SLAB, CG), BF16),
-        vmem((TOPL, SLAB, CG), BF16),
+        vmem((TOPL + 1, SLAB, CG), BF16),
         vmem((NPL, W, CG), BF16),
         vmem((LOC, W, W), BF16),
-        vmem((COLS, NPL, SLAB, CG), BF16),
+        vmem((COLS, NPL // 2, SLAB, CG), BF16),
         vmem((COLS, TOPL * SLAB, LOC * KCH), BF16),
-        vmem((COLS, 6, SLAB, CG), BF16),
-        vmem((6, W, W), BF16),
-        vmem((TOPL, W, W), BF16),
+        vmem((COLS, 4, SLAB, CG), BF16),
+        vmem((7, W, W), BF16),
+        vmem((TOPL + 1, W, W), BF16),
         vmem((TOPL, W, W), BF16),
         vmem((NPL, W, W), BF16),
         vmem((LOC, W, CG), BF16),
@@ -498,15 +524,20 @@
         vmem((3, W, CG), BF16),
         vmem((3, W, ROWS * CG), BF16),
         vmem((NPL, W, ROWS * CG), BF16),
+        vmem((4, W, W), BF16),
+        vmem((W, W), BF16),
+        vmem((3, W, ROWS * CG), BF16),
         vmem((LOC, W, CG), F32),
         vmem((LOC, W, CG), BF16),
         vmem((NPL, W, CG), BF16),
         vmem((CG, TOPL * SLAB), BF16),
         vmem((2, ROWS, CP, CG), BF16),
-        vmem((CG, TOPL * SLAB), BF16),
-        vmem((ROWS, CP, CG), BF16),
-        vmem((10, CP, W), BF16),
-        vmem((10, CP, W), BF16),
+        vmem((CG, 2 * CG), BF16),
+        vmem((ROWS, CP, 2 * CG), BF16),
+        vmem((3, CP, W), BF16),
+        vmem((3, CP, W), BF16),
+        vmem((2, CP, W), BF16),
+        vmem((3, 2, CP, W), BF16),
         vmem((CG, ROWS * CG), BF16),
         vmem((NPL, W, CG), BF16),
         vmem((NPL, W, CG), BF16),
@@ -520,8 +551,8 @@
     return pl.pallas_call(
         kernel,
         out_shape=(
-            jax.ShapeDtypeStruct((LOC, SLAB // COLS, R), F32),
-            jax.ShapeDtypeStruct((1, TOPL, SLAB // COLS, R), F32),
+            vmem((LOC, SLAB // COLS, R), F32),
+            vmem((1, TOPL, SLAB // COLS, R), F32),
         ),
         in_specs=[pl.BlockSpec(memory_space=pltpu.SMEM)] + [any_space] * 12,
         out_specs=(any_space, any_space),

time: 78.3 us -> 77.6 us (level)
  local copies, waits for them, and re-layouts: 2.23 us -> 1.29 us
    unnamed x4 -> x2, local copies, waits for them, and re-layouts: 2.23 us -> 1.29 us
where the time goes in v3:
time: 77.6 us; the launch traced here: 77.5 us
  Pallas kernels  75.6 us (97%)
  local copies, waits for them, and re-layouts  1.29 us (2%)
    pallas_call x1, Pallas kernels, per_device(): pl.pallas_call(kernel, out_shape=(vmem((LOC, SLAB // COLS, R), F32), vmem...  75.6 us

profile of v3, /device:TPU:1, one launch (start us, length us, event | category | flops | bytes accessed | tf_op | source)
XLA Modules:
  0.0 77.5 jit_solution(16614736874097222677)
XLA Ops:
  0.6 75.6 %shard_map.140 = (f32[8,8,512]{2,1,0:T(8,128)S(1)}, f32[1,4,8,512]{3,2,1,0:T(8,128)S(1)}) custom-call(s32[4]{0:T(128)} %parent.1, bf16[4,32,64]{2,1,0:T(8,128)(2,1)} %l_tree.1, bf16[8,4,32,64]{3,2,1,0:T(8,128)(2,1)} %l_path.1, bf16[15,4,32,64]{3,2,1,0:T(8,128)(2,1)} %l_top.1, bf16[4,32,64]{2,1,0:T(8,128)(2,1)} %bitcast.5, bf16[8,4,32,64]{3,2,1,0:T(8,128)(2,1)} %bitcast.4, ...), custom_call_target="tpu_custom_call" | custom-call | tf_op jit(solution)/shard_map/pallas_call | solution.py:551
  76.2 0.7 copy.17
  76.9 0.6 copy.18

commit v4 on v2

--- a/solution.py
+++ b/solution.py
@@ -36,7 +36,7 @@
     parent, l_tree, l_path, l_top, u_tree, u_path, u_top, linv_local, linv_top, uinv_local,
     uinv_top, rhs_local, rhs_top, x_local, x_path,
     st_ltree, st_lpath, st_ltop, st_utree, st_upath, st_utop, uinv_own, rhs2_own, st_rt,
-    x1, linv, lt, lp, ltp1, ltp, linvt, uinvt, uinv2, up, us, utp, ut, tree_w,
+    x1, linv, lt, lp, ltp1, ltp, linvt, uinvt, uinv2, up, us, utp, ut, tree_w, mprod, vprod, nprod,
     y, ylow, s2f, tt, rv, rt, rr, zs, zr, xp, sb2, x2low, sb1, out_l, out_p,
     lsem, ssem, rsem,
 ):
@@ -66,6 +66,12 @@
         copy.start()
         pending_sends.append(copy)
 
+    def drain(keep=0):
+        done = len(pending_sends) - keep
+        for copy in pending_sends[:done]:
+            copy.wait_send()
+        del pending_sends[:done]
+
     def await_slot(dst, slot):
         pltpu.make_async_remote_copy(
             src_ref=dst, dst_ref=dst, send_sem=ssem.at[0], recv_sem=rsem.at[slot],
@@ -135,6 +141,10 @@
 
     def lanes_of(owner):
         return pl.ds(pl.multiple_of(owner * CG, CG), CG)
+
+    c_ltree = local(l_tree, st_ltree)
+    c_lpath = local(l_path, st_lpath)
+    c_ltop = [local(l_top.at[anc[a]], st_ltop.at[a]) for a in range(3)]
 
     barrier = pltpu.get_barrier_semaphore()
 
@@ -149,21 +159,27 @@
     source = jnp.where(quarter == 0, 15, jnp.where(quarter == 1, 8, jnp.where(quarter == 2, 7, 0)))
     edge = jnp.logical_or(jnp.logical_or(g == 0, g == 7), jnp.logical_or(g == 8, g == 15))
     first_target = jnp.where(g == 0, 12, jnp.where(g == 7, 8, jnp.where(g == 8, 4, 0)))
+    greet({"gz": source})
+    greet({"gz": partners[2]})
+    greet({"gz": partners[1]})
+    for step in range(ROWS):
+        greet({"row": lax.rem(r + step, ROWS), "gz": partners[0]})
     for step in range(1, ROWS):
         greet({"row": lax.rem(r + step, ROWS)})
-    for step in range(ROWS):
-        greet({"row": lax.rem(r + step, ROWS), "gz": partners[0]})
     for step in range(1, COLS):
         greet({"col": lax.rem(c + step, COLS)})
-    greet({"gz": partners[1]})
-    greet({"gz": partners[2]})
-    greet({"gz": source})
-
+
+    pl.semaphore_wait(barrier, ROWS - 1 + ROWS + COLS - 1 + 2 + jnp.where(edge, 4, 0))
+
+    w_x1 = spread(
+        "row", lambda peer: rhs_local.at[pl.ds(0, NPL), :, my_cols],
+        lambda me: x1.at[:, aligned(me, SLAB), :],
+    )
+    f_li1, w_li1 = spread_col_shared(
+        linv_local.at[pl.ds(0, NPL), half_src], lambda o, h: linv.at[pl.ds(0, NPL), half_rows(o, h), :]
+    )
     c_x1 = local(rhs_local.at[pl.ds(0, NPL), :, my_cols], x1.at[:, my_rows, :])
     c_li1 = local(linv_local.at[pl.ds(0, NPL)], linv.at[pl.ds(0, NPL), my_k, :])
-    c_ltree = local(l_tree, st_ltree)
-    c_lpath = local(l_path, st_lpath)
-    c_ltop = [local(l_top.at[anc[a]], st_ltop.at[a]) for a in range(3)]
     c_lit = [local(linv_top.at[anc[a]], linvt.at[a, my_k, :]) for a in range(TOPL)]
     c_uit = [local(uinv_top.at[anc[a]], uinvt.at[a, my_rows, :]) for a in range(TOPL)]
     c_rt = [local(rhs_top.at[anc[a], :, my_cols], st_rt.at[a]) for a in range(TOPL)]
@@ -175,27 +191,16 @@
     c_ui2 = local(uinv_local.at[pl.ds(NPL, NPL)], uinv2.at[:, my_rows, :])
     c_uiown = local(uinv_local, uinv_own)
 
-    pl.semaphore_wait(barrier, ROWS - 1 + ROWS + COLS - 1 + 2 + jnp.where(edge, 4, 0))
-
-    w_x1 = spread(
-        "row", lambda peer: rhs_local.at[pl.ds(0, NPL), :, my_cols],
-        lambda me: x1.at[:, aligned(me, SLAB), :],
-    )
-    f_li1, w_li1 = spread_col_shared(
-        linv_local.at[pl.ds(0, NPL), half_src], lambda o, h: linv.at[pl.ds(0, NPL), half_rows(o, h), :]
-    )
-    odd = lax.rem(c, 2)
-
-    def shifted(block):
-        blank = jnp.zeros_like(block)
-        low = jnp.concatenate([block, blank], axis=-1)
-        high = jnp.concatenate([blank, block], axis=-1)
-        return jnp.where(odd == 0, low, high)
-
     c_ltree.wait()
-    for j in range(NPL):
-        lt[c, j] = shifted(st_ltree[j])
+    for b in range(NPL // 2):
+        lt[c, b] = jnp.concatenate([st_ltree[2 * b], st_ltree[2 * b + 1]], axis=-1)
     w_lt = spread("col", lambda peer: lt.at[c], lambda me: lt.at[me])
+    for copy in c_ltop:
+        copy.wait()
+    for b in range(len(L_PAIRS) // 2):
+        (a1, m1), (a2, m2) = L_PAIRS[2 * b], L_PAIRS[2 * b + 1]
+        ltp1[c, b] = jnp.concatenate([st_ltop[a1, m1], st_ltop[a2, m2]], axis=-1)
+    w_ltp1 = spread("col", lambda peer: ltp1.at[c], lambda me: ltp1.at[me])
     f_li2, w_li2 = spread_col_shared(
         linv_local.at[pl.ds(NPL, NPL), half_src], lambda o, h: linv.at[pl.ds(NPL, NPL), half_rows(o, h), :]
     )
@@ -203,11 +208,11 @@
     for m in range(TOPL):
         lp[c, pl.ds(m * SLAB, SLAB), :] = jnp.concatenate([st_lpath[k, m] for k in range(LOC)], axis=-1)
     w_lp = spread("col", lambda peer: lp.at[c], lambda me: lp.at[me])
-    for copy in c_ltop:
-        copy.wait()
-    for b, (a, m) in enumerate(L_PAIRS):
-        ltp1[c, b] = shifted(st_ltop[a, m])
-    w_ltp1 = spread("col", lambda peer: ltp1.at[c], lambda me: ltp1.at[me])
+
+    def unpaired(pieces, b):
+        half = pl.ds(b % 2 * KCH, KCH)
+        return jnp.concatenate([pieces[q, b // 2, :, half] for q in range(COLS)], axis=-1)
+
     for copy in c_lit:
         copy.wait()
     f_lit, w_lit = spread_col_shared(
@@ -217,32 +222,8 @@
         copy.wait()
     f_uit, w_uit = spread_row_shared(uinvt.at[:, my_rows, :], lambda me: uinvt.at[:, aligned(me, SLAB), :])
 
-    eye = (
-        lax.broadcasted_iota(jnp.int32, (CG, CG), 0) == lax.broadcasted_iota(jnp.int32, (CG, CG), 1)
-    ).astype(F32).astype(BF16)
-    for copy in c_rt:
-        copy.wait()
-    rt[...] = nt(eye, st_rt[...].reshape(TOPL * SLAB, CG)).astype(BF16)
-    w_rr = spread("row", lambda peer: rt.at[aligned(peer, CP), :], lambda me: rr.at[me])
-    rr[r] = rt[aligned(r, CP), :]
     c_ui2.wait()
     f_ui2, w_ui2 = spread_row_shared(uinv2.at[:, my_rows, :], lambda me: uinv2.at[:, aligned(me, SLAB), :])
-
-    eye_k = eye[0:KCH, 0:KCH]
-
-    def packed(stack):
-        return nt(eye_k, stack).astype(BF16)
-
-    for copy in c_utop:
-        copy.wait()
-    utp[0, my_k, :] = packed(jnp.concatenate([st_utop[2, 3], st_utop[0, 1], st_utop[0, 2], st_utop[0, 3]], axis=0))
-    utp[1, my_k, :] = packed(st_utop[1].reshape(CG, KCH))
-    c_utree.wait()
-    utp[2, my_k, :] = packed(st_utree[...].reshape(CG, KCH))
-    w_utp = spread("col", lambda peer: utp.at[:, my_k, :], lambda me: utp.at[:, aligned(me, KCH), :])
-    c_upath.wait()
-    for k in range(LOC):
-        up[k, my_k, :] = packed(st_upath[k].reshape(CG, KCH))
 
     c_x1.wait()
     c_li1.wait()
@@ -256,8 +237,7 @@
     w_lt()
     terms = []
     for j in range(NPL):
-        term = mm(lt[0, j] + lt[1, j], ylow[j, 0:CG, :]) + mm(lt[2, j] + lt[3, j], ylow[j, CG:W, :])
-        terms.append(term)
+        terms.append(mm(unpaired(lt, j), ylow[j]))
     c_rhs2.wait()
     for i in range(NPL):
         value = rhs2_own[i].astype(F32)
@@ -266,8 +246,37 @@
         s2f[i, my_rows, :] = value.astype(BF16)
     w_s2 = spread("row", lambda peer: s2f.at[:, my_rows, :], lambda me: s2f.at[:, aligned(me, SLAB), :])
 
+    eye = (
+        lax.broadcasted_iota(jnp.int32, (CG, CG), 0) == lax.broadcasted_iota(jnp.int32, (CG, CG), 1)
+    ).astype(F32).astype(BF16)
+    for copy in c_rt:
+        copy.wait()
+    rt[...] = nt(eye, st_rt[...].reshape(TOPL * SLAB, CG)).astype(BF16)
+    w_rr = spread("row", lambda peer: rt.at[aligned(peer, CP), :], lambda me: rr.at[me])
+    rr[r] = rt[aligned(r, CP), :]
+    w_ltp1()
+    for b in range(len(L_PAIRS)):
+        ltp[b, my_rows, :] = unpaired(ltp1, b)
+    f_ltp, w_ltp = spread_row_shared(ltp.at[:, my_rows, :], lambda me: ltp.at[:, aligned(me, SLAB), :])
+    f_li2()
+
+    eye_k = eye[0:KCH, 0:KCH]
+
+    def packed(stack):
+        return nt(eye_k, stack).astype(BF16)
+
+    for copy in c_utop:
+        copy.wait()
+    utp[0, my_k, :] = packed(jnp.concatenate([st_utop[2, 3], st_utop[0, 1], st_utop[0, 2], st_utop[0, 3]], axis=0))
+    utp[1, my_k, :] = packed(st_utop[1].reshape(CG, KCH))
+    c_utree.wait()
+    utp[2, my_k, :] = packed(st_utree[...].reshape(CG, KCH))
+    w_utp = spread("col", lambda peer: utp.at[:, my_k, :], lambda me: utp.at[:, aligned(me, KCH), :])
+    c_upath.wait()
+    for k in range(LOC):
+        up[k, my_k, :] = packed(st_upath[k].reshape(CG, KCH))
+
     w_up = spread("col", lambda peer: up.at[:, my_k, :], lambda me: up.at[:, aligned(me, KCH), :])
-    f_li2()
     w_lp()
     toward = jnp.zeros((TOPL * SLAB, CG), F32)
     for q in range(COLS):
@@ -300,13 +309,9 @@
             await_slot(rv.at[0, sender], base + step)
             await_slot(rv.at[1, sender], base + ROWS + step)
 
-    w_ltp1()
-    for b in range(len(L_PAIRS)):
-        ltp[b, my_rows, :] = jnp.concatenate([ltp1[0, b] + ltp1[1, b], ltp1[2, b] + ltp1[3, b]], axis=-1)
-    f_ltp, w_ltp = spread_row_shared(ltp.at[:, my_rows, :], lambda me: ltp.at[:, aligned(me, SLAB), :])
     f_lit()
 
-    slot_of_lane = lax.broadcasted_iota(jnp.int32, (CP, CG), 1) // SLAB
+    slot_of_lane = lax.shift_right_logical(lax.broadcasted_iota(jnp.int32, (CP, CG), 1), 5)
 
     def by_level(tiles, m):
         halves = []
@@ -326,10 +331,10 @@
     w_utp()
     f_ut, w_ut = spread_row_shared(utp, lambda me: ut.at[:, :, lanes_of(me)])
     c_ut = local(utp, ut.at[:, :, lanes_of(r)])
+    f_ltp()
     w_rv()
     rv_tiles = [rv[0, q].astype(F32) + rv[1, q].astype(F32) for q in range(ROWS)]
     pend = [by_level(rv_tiles, m) for m in range(TOPL)]
-    f_ltp()
     w_lit()
     w_ltp()
 
@@ -361,37 +366,50 @@
             if a == 1:
                 f_uit()
                 f_ui2()
+                for n, (b, below) in enumerate(((3, 1), (4, 1), (5, 2))):
+                    mprod[n] = mm(ltp[b], linvt[below]).astype(BF16)
+            if a == 2:
                 w_up()
                 w_us = spread(
                     "row", lambda peer: up.at[:, aligned(peer, SLAB), :], lambda me: us.at[:, :, lanes_of(me)]
                 )
                 c_us = local(up.at[:, my_rows, :], us.at[:, :, lanes_of(r)])
+                w_uit()
+                vprod[...] = mm(uinvt[TOPL - 1], linvt[TOPL - 1]).astype(BF16)
+                known_x = [nt(top_y[n].astype(BF16), uinvt[n]) for n in range(2)]
             if a == 3:
+                known_x.append(nt(top_y[2].astype(BF16), uinvt[2]))
                 f_ut()
+                c_ut.wait()
+                w_ut()
+                for n, tile in enumerate((0, 1, 0)):
+                    nprod[n] = mm(uinvt[n], ut[tile]).astype(BF16)
             await_slot(zr.at[place], slot)
             for m in range(a, TOPL):
                 pend[m] = pend[m] + zr[base + m - a].astype(F32)
-        solved = nt((top_rhs[a] - pend[a]).astype(BF16), linvt[a])
-        top_y.append(solved)
-        low = solved.astype(BF16)
-        for b, (below, m) in enumerate(L_PAIRS):
-            if below == a:
-                pend[m] = pend[m] + nt(low, ltp[b])
-
-    w_uit()
-    c_ut.wait()
-    w_ut()
+        low = (top_rhs[a] - pend[a]).astype(BF16)
+        if a == 0:
+            top_y.append(nt(low, linvt[a]))
+            low = top_y[0].astype(BF16)
+            for b in range(3):
+                pend[b + 1] = pend[b + 1] + nt(low, ltp[b])
+        elif a < TOPL - 1:
+            for m in range(a + 1, TOPL):
+                pend[m] = pend[m] + nt(low, mprod[m - 2 if a == 1 else 2])
+            top_y.append(nt(low, linvt[a]))
+        else:
+            known_x.append(nt(low, vprod[...]))
+
     tiles = [jnp.zeros((CP, CG), F32) for _ in range(ROWS)]
     for a in reversed(range(TOPL)):
-        value = top_y[a]
+        solved = known_x[a]
         if a < TOPL - 1:
             if a == 2:
                 known = [pltpu.roll(tile, SLAB, 1) for tile in tiles]
             else:
                 known = tiles
             above = jnp.concatenate(known, axis=-1).astype(BF16)
-            value = value - nt(above, ut[0 if a != 1 else 1])
-        solved = nt(value.astype(BF16), uinvt[a])
+            solved = solved - nt(above, nprod[a])
         for q in range(2):
             half = solved[:, q * CG:(q + 1) * CG]
             for s in range(4):
@@ -401,9 +419,11 @@
     xp[my_cp, :] = jnp.concatenate(tiles, axis=-1).astype(BF16)
     w_xp = spread("row", lambda peer: xp.at[my_cp, :], lambda me: xp.at[aligned(me, CP), :])
 
-    lane_slot = lax.rem(lax.broadcasted_iota(jnp.int32, (W, ROWS * CG), 1) // SLAB, NPL)
+    lane_slot = lax.shift_right_logical(lax.broadcasted_iota(jnp.int32, (8, CG), 1), 5)
     for j in range(NPL):
-        tree_w[j] = jnp.where(lane_slot == j, ut[2], jnp.zeros((W, ROWS * CG), BF16))
+        mask = jnp.where(lane_slot == j, 1.0, 0.0).astype(F32)[0:1, :].astype(BF16)
+        for q in range(ROWS):
+            tree_w[j, :, q * CG:(q + 1) * CG] = ut[2, :, q * CG:(q + 1) * CG] * mask
     c_us.wait()
     w_us()
     w_xp()
@@ -412,12 +432,12 @@
     for i in range(NPL):
         value = y[NPL + i, my_rows, :] - path_term2[i * SLAB:(i + 1) * SLAB, :]
         sb2[i, my_rows, :] = value.astype(BF16)
-    w_sb2 = spread("row", lambda peer: sb2.at[:, my_rows, :], lambda me: sb2.at[:, aligned(me, SLAB), :])
+    f_sb2, w_sb2 = spread_row_shared(sb2.at[:, my_rows, :], lambda me: sb2.at[:, aligned(me, SLAB), :])
     path_term1 = nt(us[0:NPL].reshape(NPL * SLAB, ROWS * CG), path)
     for j in range(NPL):
         value = y[j, my_rows, :] - path_term1[j * SLAB:(j + 1) * SLAB, :]
         sb1[j, my_rows, :] = value.astype(BF16)
-    w_sb1 = spread("row", lambda peer: sb1.at[:, my_rows, :], lambda me: sb1.at[:, aligned(me, SLAB), :])
+    f_sb1, w_sb1 = spread_row_shared(sb1.at[:, my_rows, :], lambda me: sb1.at[:, aligned(me, SLAB), :])
     own_path = nt(eye, xp[:, lanes_of(r)])
     for m in range(TOPL):
         out_p[m] = own_path[m * SLAB:(m + 1) * SLAB, :]
@@ -433,6 +453,15 @@
 
     w_ui2()
     c_uiown.wait()
+    drain(14)
+
+    @pl.when(edge)
+    def _():
+        for copy in last_sends:
+            copy.wait_send()
+
+    f_sb2()
+    f_sb1()
     w_sb2()
     for i in range(NPL):
         x2low[i] = mm(uinv2[i], sb2[i]).astype(BF16)
@@ -456,16 +485,12 @@
     w_out1, c_out1 = send_out(0)
     w_outp()
     w_out2()
+    c_outp.wait()
+    c_out2.wait()
+    drain(COLS - 1)
     w_out1()
-    for copy in (c_outp, c_out2, c_out1):
-        copy.wait()
-    for copy in pending_sends:
-        copy.wait_send()
-
-    @pl.when(edge)
-    def _():
-        for copy in last_sends:
-            copy.wait_send()
+    c_out1.wait()
+    drain()
 
 
 def per_device(*arrays):
@@ -486,9 +511,9 @@
         vmem((TOPL, SLAB, CG), BF16),
         vmem((NPL, W, CG), BF16),
         vmem((LOC, W, W), BF16),
-        vmem((COLS, NPL, SLAB, CG), BF16),
+        vmem((COLS, NPL // 2, SLAB, CG), BF16),
         vmem((COLS, TOPL * SLAB, LOC * KCH), BF16),
-        vmem((COLS, 6, SLAB, CG), BF16),
+        vmem((COLS, 3, SLAB, CG), BF16),
         vmem((6, W, W), BF16),
         vmem((TOPL, W, W), BF16),
         vmem((TOPL, W, W), BF16),
@@ -498,6 +523,9 @@
         vmem((3, W, CG), BF16),
         vmem((3, W, ROWS * CG), BF16),
         vmem((NPL, W, ROWS * CG), BF16),
+        vmem((3, W, W), BF16),
+        vmem((W, W), BF16),
+        vmem((3, W, ROWS * CG), BF16),
         vmem((LOC, W, CG), F32),
         vmem((LOC, W, CG), BF16),
         vmem((NPL, W, CG), BF16),
@@ -520,8 +548,8 @@
     return pl.pallas_call(
         kernel,
         out_shape=(
-            jax.ShapeDtypeStruct((LOC, SLAB // COLS, R), F32),
-            jax.ShapeDtypeStruct((1, TOPL, SLAB // COLS, R), F32),
+            vmem((LOC, SLAB // COLS, R), F32),
+            vmem((1, TOPL, SLAB // COLS, R), F32),
         ),
         in_specs=[pl.BlockSpec(memory_space=pltpu.SMEM)] + [any_space] * 12,
         out_specs=(any_space, any_space),

time: 78.3 us -> 73.5 us (0.939)
  Pallas kernels: 75.2 us -> 71.4 us
  local copies, waits for them, and re-layouts: 2.23 us -> 1.29 us
    pallas_call x1, Pallas kernels: 75.2 us -> 71.4 us  [per_device(): pl.pallas_call(kernel, out_shape=(vmem((LOC, SLAB // COLS, R), F32), vmem...]
    unnamed x4 -> x2, local copies, waits for them, and re-layouts: 2.23 us -> 1.29 us
where the time goes in v4:
time: 73.5 us; the launch traced here: 73.4 us
  Pallas kernels  71.4 us (97%)
  local copies, waits for them, and re-layouts  1.29 us (2%)
    pallas_call x1, Pallas kernels, per_device(): pl.pallas_call(kernel, out_shape=(vmem((LOC, SLAB // COLS, R), F32), vmem...  71.4 us

profile of v4, /device:TPU:1, one launch (start us, length us, event | category | flops | bytes accessed | tf_op | source)
XLA Modules:
  0.0 73.4 jit_solution(17227600624130841399)
XLA Ops:
  0.6 71.4 %shard_map.140 = (f32[8,8,512]{2,1,0:T(8,128)S(1)}, f32[1,4,8,512]{3,2,1,0:T(8,128)S(1)}) custom-call(s32[4]{0:T(128)} %parent.1, bf16[4,32,64]{2,1,0:T(8,128)(2,1)} %l_tree.1, bf16[8,4,32,64]{3,2,1,0:T(8,128)(2,1)} %l_path.1, bf16[15,4,32,64]{3,2,1,0:T(8,128)(2,1)} %l_top.1, bf16[4,32,64]{2,1,0:T(8,128)(2,1)} %bitcast.5, bf16[8,4,32,64]{3,2,1,0:T(8,128)(2,1)} %bitcast.4, ...), custom_call_target="tpu_custom_call" | custom-call | tf_op jit(solution)/shard_map/pallas_call | solution.py:548
  72.1 0.7 copy.17
  72.7 0.6 copy.18

commit v5 on v4

--- a/solution.py
+++ b/solution.py
@@ -18,6 +18,7 @@
 CP = CG // ROWS
 L_PAIRS = ((0, 1), (0, 2), (0, 3), (1, 2), (1, 3), (2, 3))
 Z_BASE = (0, 4, 7, 9)
+FAR_FIRST = {8: (4, 3, 5, 2, 6, 1, 7), 4: (2, 1, 3)}
 
 
 def nt(a, b):
@@ -81,7 +82,7 @@
     def spread(axis, src_of, dst_of):
         me, size = (r, ROWS) if axis == "row" else (c, COLS)
         base = take("r", size)
-        for step in range(1, size):
+        for step in FAR_FIRST[size]:
             peer = lax.rem(me + step, size)
             remote(src_of(peer), dst_of(me), base + step, {axis: peer})
 
@@ -142,9 +143,6 @@
     def lanes_of(owner):
         return pl.ds(pl.multiple_of(owner * CG, CG), CG)
 
-    c_ltree = local(l_tree, st_ltree)
-    c_lpath = local(l_path, st_lpath)
-    c_ltop = [local(l_top.at[anc[a]], st_ltop.at[a]) for a in range(3)]
 
     barrier = pltpu.get_barrier_semaphore()
 
@@ -159,15 +157,19 @@
     source = jnp.where(quarter == 0, 15, jnp.where(quarter == 1, 8, jnp.where(quarter == 2, 7, 0)))
     edge = jnp.logical_or(jnp.logical_or(g == 0, g == 7), jnp.logical_or(g == 8, g == 15))
     first_target = jnp.where(g == 0, 12, jnp.where(g == 7, 8, jnp.where(g == 8, 4, 0)))
+    for step in range(1, COLS):
+        greet({"col": lax.rem(c + step, COLS)})
+    for step in range(1, ROWS):
+        greet({"row": lax.rem(r + step, ROWS)})
     greet({"gz": source})
     greet({"gz": partners[2]})
     greet({"gz": partners[1]})
     for step in range(ROWS):
         greet({"row": lax.rem(r + step, ROWS), "gz": partners[0]})
-    for step in range(1, ROWS):
-        greet({"row": lax.rem(r + step, ROWS)})
-    for step in range(1, COLS):
-        greet({"col": lax.rem(c + step, COLS)})
+
+    c_ltree = local(l_tree, st_ltree)
+    c_lpath = local(l_path, st_lpath)
+    c_ltop = [local(l_top.at[anc[a]], st_ltop.at[a]) for a in range(3)]
 
     pl.semaphore_wait(barrier, ROWS - 1 + ROWS + COLS - 1 + 2 + jnp.where(edge, 4, 0))
 
@@ -200,7 +202,7 @@
     for b in range(len(L_PAIRS) // 2):
         (a1, m1), (a2, m2) = L_PAIRS[2 * b], L_PAIRS[2 * b + 1]
         ltp1[c, b] = jnp.concatenate([st_ltop[a1, m1], st_ltop[a2, m2]], axis=-1)
-    w_ltp1 = spread("col", lambda peer: ltp1.at[c], lambda me: ltp1.at[me])
+    w_ltp1a = spread("col", lambda peer: ltp1.at[c, pl.ds(0, 2)], lambda me: ltp1.at[me, pl.ds(0, 2)])
     f_li2, w_li2 = spread_col_shared(
         linv_local.at[pl.ds(NPL, NPL), half_src], lambda o, h: linv.at[pl.ds(NPL, NPL), half_rows(o, h), :]
     )
@@ -215,8 +217,13 @@
 
     for copy in c_lit:
         copy.wait()
+    first, rest = pl.ds(0, 1), pl.ds(1, TOPL - 1)
+    f_lit0, w_lit0 = spread_col_shared(
+        linvt.at[first, half_rows(c, core), :], lambda o, h: linvt.at[first, half_rows(o, h), :]
+    )
+    w_ltp1b = spread("col", lambda peer: ltp1.at[c, pl.ds(2, 1)], lambda me: ltp1.at[me, pl.ds(2, 1)])
     f_lit, w_lit = spread_col_shared(
-        linvt.at[:, half_rows(c, core), :], lambda o, h: linvt.at[:, half_rows(o, h), :]
+        linvt.at[rest, half_rows(c, core), :], lambda o, h: linvt.at[rest, half_rows(o, h), :]
     )
     for copy in c_uit:
         copy.wait()
@@ -254,10 +261,13 @@
     rt[...] = nt(eye, st_rt[...].reshape(TOPL * SLAB, CG)).astype(BF16)
     w_rr = spread("row", lambda peer: rt.at[aligned(peer, CP), :], lambda me: rr.at[me])
     rr[r] = rt[aligned(r, CP), :]
-    w_ltp1()
-    for b in range(len(L_PAIRS)):
+    w_ltp1a()
+    for b in range(4):
         ltp[b, my_rows, :] = unpaired(ltp1, b)
-    f_ltp, w_ltp = spread_row_shared(ltp.at[:, my_rows, :], lambda me: ltp.at[:, aligned(me, SLAB), :])
+    lower, upper = pl.ds(0, 3), pl.ds(3, 3)
+    f_ltpa, w_ltpa = spread_row_shared(
+        ltp.at[lower, my_rows, :], lambda me: ltp.at[lower, aligned(me, SLAB), :]
+    )
     f_li2()
 
     eye_k = eye[0:KCH, 0:KCH]
@@ -295,11 +305,11 @@
         toward = toward + mm(lp[q, :, NPL * KCH:LOC * KCH], block)
     tt[...] = nt(eye, toward.astype(BF16)).astype(BF16)
     base = take("r", 2 * ROWS)
-    remote(tt.at[aligned(r, CP), :], rv.at[1, r], base + ROWS, {"gz": partners[0]})
-    for step in range(1, ROWS):
+    for step in FAR_FIRST[ROWS]:
         peer = lax.rem(r + step, ROWS)
         remote(tt.at[aligned(peer, CP), :], rv.at[1, r], base + ROWS + step, {"row": peer, "gz": partners[0]})
         remote(tt.at[aligned(peer, CP), :], rv.at[0, r], base + step, {"row": peer})
+    remote(tt.at[aligned(r, CP), :], rv.at[1, r], base + ROWS, {"gz": partners[0]})
     rv[0, r] = tt[aligned(r, CP), :]
 
     def w_rv():
@@ -309,7 +319,13 @@
             await_slot(rv.at[0, sender], base + step)
             await_slot(rv.at[1, sender], base + ROWS + step)
 
-    f_lit()
+    f_lit0()
+    w_ltp1b()
+    for b in range(4, 6):
+        ltp[b, my_rows, :] = unpaired(ltp1, b)
+    f_ltpb, w_ltpb = spread_row_shared(
+        ltp.at[upper, my_rows, :], lambda me: ltp.at[upper, aligned(me, SLAB), :]
+    )
 
     slot_of_lane = lax.shift_right_logical(lax.broadcasted_iota(jnp.int32, (CP, CG), 1), 5)
 
@@ -331,12 +347,12 @@
     w_utp()
     f_ut, w_ut = spread_row_shared(utp, lambda me: ut.at[:, :, lanes_of(me)])
     c_ut = local(utp, ut.at[:, :, lanes_of(r)])
-    f_ltp()
+    f_ltpa()
     w_rv()
     rv_tiles = [rv[0, q].astype(F32) + rv[1, q].astype(F32) for q in range(ROWS)]
     pend = [by_level(rv_tiles, m) for m in range(TOPL)]
-    w_lit()
-    w_ltp()
+    w_lit0()
+    w_ltpa()
 
     top_y = []
     for a in range(TOPL):
@@ -364,8 +380,12 @@
                         copy.start()
 
             if a == 1:
+                f_lit()
+                f_ltpb()
                 f_uit()
                 f_ui2()
+                w_lit()
+                w_ltpb()
                 for n, (b, below) in enumerate(((3, 1), (4, 1), (5, 2))):
                     mprod[n] = mm(ltp[b], linvt[below]).astype(BF16)
             if a == 2:

time: 73.5 us -> 72.7 us (0.989)
  Pallas kernels: 71.4 us -> 70.6 us
    pallas_call x1, Pallas kernels: 71.4 us -> 70.6 us  [per_device(): pl.pallas_call(kernel, out_shape=(vmem((LOC, SLAB // COLS, R), F32), vmem...]
where the time goes in v5:
time: 72.7 us; the launch traced here: 72.6 us
  Pallas kernels  70.6 us (97%)
  local copies, waits for them, and re-layouts  1.29 us (2%)
    pallas_call x1, Pallas kernels, per_device(): pl.pallas_call(kernel, out_shape=(vmem((LOC, SLAB // COLS, R), F32), vmem...  70.6 us

profile of v5, /device:TPU:1, one launch (start us, length us, event | category | flops | bytes accessed | tf_op | source)
XLA Modules:
  0.0 72.6 jit_solution(16078150189435664745)
XLA Ops:
  0.6 70.6 %shard_map.140 = (f32[8,8,512]{2,1,0:T(8,128)S(1)}, f32[1,4,8,512]{3,2,1,0:T(8,128)S(1)}) custom-call(s32[4]{0:T(128)} %parent.1, bf16[4,32,64]{2,1,0:T(8,128)(2,1)} %l_tree.1, bf16[8,4,32,64]{3,2,1,0:T(8,128)(2,1)} %l_path.1, bf16[15,4,32,64]{3,2,1,0:T(8,128)(2,1)} %l_top.1, bf16[4,32,64]{2,1,0:T(8,128)(2,1)} %bitcast.5, bf16[8,4,32,64]{3,2,1,0:T(8,128)(2,1)} %bitcast.4, ...), custom_call_target="tpu_custom_call" | custom-call | tf_op jit(solution)/shard_map/pallas_call | solution.py:568
  71.3 0.7 copy.17
  71.9 0.6 copy.18

commit v6 on v5

--- a/solution.py
+++ b/solution.py
@@ -37,7 +37,7 @@
     parent, l_tree, l_path, l_top, u_tree, u_path, u_top, linv_local, linv_top, uinv_local,
     uinv_top, rhs_local, rhs_top, x_local, x_path,
     st_ltree, st_lpath, st_ltop, st_utree, st_upath, st_utop, uinv_own, rhs2_own, st_rt,
-    x1, linv, lt, lp, ltp1, ltp, linvt, uinvt, uinv2, up, us, utp, ut, tree_w, mprod, vprod, nprod,
+    x1, linv, lt, lp, ltp1, ltp, linvt, uinvt, uinv2, up, us, utp, ut, tree_w, mprod, vprod,
     y, ylow, s2f, tt, rv, rt, rr, zs, zr, xp, sb2, x2low, sb1, out_l, out_p,
     lsem, ssem, rsem,
 ):
@@ -156,7 +156,8 @@
     quarter = g // 4
     source = jnp.where(quarter == 0, 15, jnp.where(quarter == 1, 8, jnp.where(quarter == 2, 7, 0)))
     edge = jnp.logical_or(jnp.logical_or(g == 0, g == 7), jnp.logical_or(g == 8, g == 15))
-    first_target = jnp.where(g == 0, 12, jnp.where(g == 7, 8, jnp.where(g == 8, 4, 0)))
+    far_target = jnp.where(g == 0, 12, jnp.where(g == 7, 11, jnp.where(g == 8, 4, 3)))
+    inward = 1 - 2 * lax.rem(g, 2)
     for step in range(1, COLS):
         greet({"col": lax.rem(c + step, COLS)})
     for step in range(1, ROWS):
@@ -251,7 +252,7 @@
         for j in range(NPL):
             value = value - jnp.where(parent[j] == i, 1.0, 0.0).astype(F32) * terms[j]
         s2f[i, my_rows, :] = value.astype(BF16)
-    w_s2 = spread("row", lambda peer: s2f.at[:, my_rows, :], lambda me: s2f.at[:, aligned(me, SLAB), :])
+    f_s2, w_s2 = spread_row_shared(s2f.at[:, my_rows, :], lambda me: s2f.at[:, aligned(me, SLAB), :])
 
     eye = (
         lax.broadcasted_iota(jnp.int32, (CG, CG), 0) == lax.broadcasted_iota(jnp.int32, (CG, CG), 1)
@@ -287,6 +288,7 @@
         up[k, my_k, :] = packed(st_upath[k].reshape(CG, KCH))
 
     w_up = spread("col", lambda peer: up.at[:, my_k, :], lambda me: up.at[:, aligned(me, KCH), :])
+    f_s2()
     w_lp()
     toward = jnp.zeros((TOPL * SLAB, CG), F32)
     for q in range(COLS):
@@ -369,7 +371,7 @@
                 last_sends = [
                     pltpu.make_async_remote_copy(
                         src_ref=zs.at[place], dst_ref=zr.at[place], send_sem=ssem.at[take("s")],
-                        recv_sem=rsem.at[slot], device_id={"gz": first_target + step}, device_id_type=MESH,
+                        recv_sem=rsem.at[slot], device_id={"gz": far_target + inward * step}, device_id_type=MESH,
                     )
                     for step in range(4)
                 ]
@@ -400,10 +402,6 @@
             if a == 3:
                 known_x.append(nt(top_y[2].astype(BF16), uinvt[2]))
                 f_ut()
-                c_ut.wait()
-                w_ut()
-                for n, tile in enumerate((0, 1, 0)):
-                    nprod[n] = mm(uinvt[n], ut[tile]).astype(BF16)
             await_slot(zr.at[place], slot)
             for m in range(a, TOPL):
                 pend[m] = pend[m] + zr[base + m - a].astype(F32)
@@ -420,6 +418,8 @@
         else:
             known_x.append(nt(low, vprod[...]))
 
+    c_ut.wait()
+    w_ut()
     tiles = [jnp.zeros((CP, CG), F32) for _ in range(ROWS)]
     for a in reversed(range(TOPL)):
         solved = known_x[a]
@@ -429,7 +429,7 @@
             else:
                 known = tiles
             above = jnp.concatenate(known, axis=-1).astype(BF16)
-            solved = solved - nt(above, nprod[a])
+            solved = solved - nt(nt(above, ut[0 if a != 1 else 1]).astype(BF16), uinvt[a])
         for q in range(2):
             half = solved[:, q * CG:(q + 1) * CG]
             for s in range(4):
@@ -545,7 +545,6 @@
         vmem((NPL, W, ROWS * CG), BF16),
         vmem((3, W, W), BF16),
         vmem((W, W), BF16),
-        vmem((3, W, ROWS * CG), BF16),
         vmem((LOC, W, CG), F32),
         vmem((LOC, W, CG), BF16),
         vmem((NPL, W, CG), BF16),

time: 72.7 us -> 73.3 us (level)
  no operation moved by 1% of the time
where the time goes in v6:
time: 73.3 us; the launch traced here: 73.2 us
  Pallas kernels  71.2 us (97%)
  local copies, waits for them, and re-layouts  1.29 us (2%)
    pallas_call x1, Pallas kernels, per_device(): pl.pallas_call(kernel, out_shape=(vmem((LOC, SLAB // COLS, R), F32), vmem...  71.2 us

profile of v6, /device:TPU:1, one launch (start us, length us, event | category | flops | bytes accessed | tf_op | source)
XLA Modules:
  0.0 73.2 jit_solution(7027858269794288619)
XLA Ops:
  0.6 71.2 %shard_map.140 = (f32[8,8,512]{2,1,0:T(8,128)S(1)}, f32[1,4,8,512]{3,2,1,0:T(8,128)S(1)}) custom-call(s32[4]{0:T(128)} %parent.1, bf16[4,32,64]{2,1,0:T(8,128)(2,1)} %l_tree.1, bf16[8,4,32,64]{3,2,1,0:T(8,128)(2,1)} %l_path.1, bf16[15,4,32,64]{3,2,1,0:T(8,128)(2,1)} %l_top.1, bf16[4,32,64]{2,1,0:T(8,128)(2,1)} %bitcast.5, bf16[8,4,32,64]{3,2,1,0:T(8,128)(2,1)} %bitcast.4, ...), custom_call_target="tpu_custom_call" | custom-call | tf_op jit(solution)/shard_map/pallas_call | solution.py:567
  71.9 0.7 copy.17
  72.5 0.6 copy.18
